TPU v7x, 256 devices: a whole 4x4x8 slice. The times are simulated.
256 devices in a mesh: section: 4 (over z_lo, core), replica: 64 (over z_hi, y, x).
Axes of the slice: x: 4, y: 4, z: 8 (z_hi: 4, z_lo: 2; z = z_hi * 2 + z_lo), core: 2. Of those that a mesh axis runs over, the one named last changes fastest.
Arguments:
- embeddings: bfloat16 [64, 4, 32, 2048], P('replica'), may hold values from -6 to 6
- cotangent: bfloat16 [64, 4, 32, 2048], P('replica'), may hold values from -6 to 6
- plan: int32 [64, 4], P('replica'), may hold values from 0 to 3, each once within a row
- doc_ids: int32 [64, 4, 32], P('replica'), may hold values from 0 to 3, never falling along the last dimension, each value on 1 to 16 neighbouring positions
- norm_gain: bfloat16 [4, 2048], P('section'), may hold values from 0.099609375 to 1.8984375
- w_query: bfloat16 [4, 2048, 1024], P('section', 'replica'), may hold values from -0.125 to 0.125
- w_out: bfloat16 [4, 1024, 2048], P('section', 'replica'), may hold values from -0.1875 to 0.1875
- kv_stash: bfloat16 [4, 2048, 512], P('section'), may hold values from -0.125 to 0.125
- kv_now: bfloat16 [4, 2048, 512], P('section'), may hold values from -0.125 to 0.125
- adam_m: bfloat16 [4, 2048, 512], P('section', 'replica'), may hold values from -3 to 3
- adam_v: bfloat16 [4, 2048, 512], P('section', 'replica'), may hold values from 0.25 to 4
Outputs:
- stash_next: bfloat16 [4, 2048, 512], P('section')
- current_next: bfloat16 [4, 2048, 512], P('section')
- moment_first: bfloat16 [4, 2048, 512], P('section', 'replica')
- moment_second: bfloat16 [4, 2048, 512], P('section', 'replica')
Inputs may be any that keep to these rules, and one draw needn't show every extreme that they name: `plan`: each row orders the 4 sequences of a replica, each once. `doc_ids`: never falling along a sequence; each document has 1 to 16 tokens.
All inputs are finite; a program needn't handle non-finite values.
Results may differ from a plain program's by a relative error of at most 0.024.
Values may be sent and summed in bfloat16 or wider, within the bound.
A program may use at most 128 MiB of HBM per device.

v0:
```python
import jax
import jax.numpy as jnp
from jax import lax
from jax.sharding import PartitionSpec as P

HEAD = 64
MICRO = 2


beta_first = 0.9
beta_second = 0.999
learn_rate = 0.003
adam_eps = 1e-08
norm_eps = 1e-05


def shifted(x, axis, by):
    devices = lax.axis_size(axis)
    pairs = [(i, i + by) for i in range(devices) if 0 <= i + by < devices]
    return lax.ppermute(x, axis, pairs)


def pre_norm(wide_hidden, gain):
    return (
        wide_hidden
        * lax.rsqrt(jnp.mean(wide_hidden * wide_hidden, axis=-1, keepdims=True) + norm_eps)
        * gain.astype(jnp.float32)
    )


def attend_core(query_wide, paired_wide, doc_row):
    length = query_wide.shape[0]
    queries = query_wide.astype(jnp.bfloat16)
    paired = paired_wide.astype(jnp.bfloat16)
    kv_heads = paired.shape[1] // (2 * HEAD)
    query_heads = queries.reshape(length, kv_heads, -1, HEAD).astype(jnp.float32)
    keys = paired[:, : kv_heads * HEAD].reshape(length, kv_heads, HEAD).astype(jnp.float32)
    values = paired[:, kv_heads * HEAD :].reshape(length, kv_heads, HEAD).astype(jnp.float32)
    scores = jnp.einsum("tgsd,ugd->gstu", query_heads, keys) * HEAD ** (-0.5)
    places = jnp.arange(length)
    allowed = (places[:, None] >= places[None, :]) & (doc_row[:, None] == doc_row[None, :])
    weight = jnp.where(allowed, jnp.exp(scores), 0.0)
    probs = (weight / jnp.sum(weight, axis=-1, keepdims=True)).astype(jnp.bfloat16)
    mixed = jnp.einsum("gstu,ugd->tgsd", probs.astype(jnp.float32), values)
    return mixed.reshape(length, -1)


def project_in(hidden, weights, query_weight, gain):
    wide_hidden = hidden.astype(jnp.float32)
    normed = pre_norm(wide_hidden, gain).astype(jnp.bfloat16)
    paired = jnp.dot(normed, weights, preferred_element_type=jnp.float32).astype(jnp.bfloat16)
    queries = jnp.dot(normed, query_weight, preferred_element_type=jnp.float32).astype(jnp.bfloat16)
    return (wide_hidden, normed, paired, queries)


def forward(hidden, weights, query_weight, output_weight, gain, doc_row):
    wide_hidden, normed, paired, queries = project_in(hidden, weights, query_weight, gain)
    mixed = attend_core(queries.astype(jnp.float32), paired.astype(jnp.float32), doc_row).astype(
        jnp.bfloat16
    )
    result = wide_hidden + jnp.dot(mixed, output_weight, preferred_element_type=jnp.float32)
    return result.astype(jnp.bfloat16)


def backward(hidden, upstream, weights, query_weight, output_weight, gain, doc_row):
    wide_hidden, normed, paired, queries = project_in(hidden, weights, query_weight, gain)
    mixed_grad = lax.dot_general(
        upstream, output_weight, (((1,), (1,)), ((), ())), preferred_element_type=jnp.float32
    )

    def local_core(query_in, paired_in):
        return attend_core(query_in, paired_in, doc_row)

    unused, pull_back = jax.vjp(local_core, queries.astype(jnp.float32), paired.astype(jnp.float32))
    grad_query, grad_paired = pull_back(mixed_grad)
    key_grad = grad_paired.astype(jnp.bfloat16)
    query_grad = grad_query.astype(jnp.bfloat16)
    grad_normed = lax.dot_general(
        query_grad, query_weight, (((1,), (1,)), ((), ())), preferred_element_type=jnp.float32
    )
    grad_normed = grad_normed + lax.dot_general(
        key_grad, weights, (((1,), (1,)), ((), ())), preferred_element_type=jnp.float32
    )

    def local_norm(hidden_in):
        return pre_norm(hidden_in, gain)

    unused_norm, norm_back = jax.vjp(local_norm, wide_hidden)
    (grad_through,) = norm_back(grad_normed)
    return ((upstream.astype(jnp.float32) + grad_through).astype(jnp.bfloat16), normed, key_grad)


def adam_update(weights, first, second, gradient):
    first_new = beta_first * first.astype(jnp.float32) + (1.0 - beta_first) * gradient
    second_new = (
        beta_second * second.astype(jnp.float32) + (1.0 - beta_second) * gradient * gradient
    )
    moved = weights.astype(jnp.float32) - learn_rate * first_new / (jnp.sqrt(second_new) + adam_eps)
    return (
        moved.astype(jnp.bfloat16),
        first_new.astype(jnp.bfloat16),
        second_new.astype(jnp.bfloat16),
    )


def reduce_rows(layer_total):
    return lax.psum_scatter(layer_total, "replica", scatter_dimension=0, tiled=True)


def body(
    embeddings,
    cotangent,
    plan,
    doc_ids,
    norm_gain,
    w_query,
    w_out,
    kv_stash,
    kv_now,
    adam_m,
    adam_v,
):
    query_full, output_full = (
        lax.all_gather(w_query, "replica", axis=1, tiled=True),
        lax.all_gather(w_out, "replica", axis=1, tiled=True),
    )
    query_weight = query_full[0]
    output_weight = output_full[0]
    gain = norm_gain[0]
    sections = lax.axis_size("section")
    position = lax.axis_index("section")
    tick_count = sections + MICRO - 1
    embed_rows = embeddings[0]
    cot_rows = cotangent[0]
    order = plan[0]
    doc_rows = doc_ids[0]
    length = embed_rows.shape[1]
    width = embed_rows.shape[2]

    def run_step(which_step, weights):
        pair_width = weights.shape[1]
        stored = jnp.zeros((MICRO, length, width), jnp.bfloat16)
        incoming = jnp.zeros((length, width), jnp.bfloat16)
        for counter in range(tick_count):
            micro_index = counter - position
            active = (micro_index >= 0) & (micro_index < MICRO)
            clipped = jnp.clip(micro_index, 0, MICRO - 1)
            chosen = lax.dynamic_index_in_dim(
                order, which_step * MICRO + clipped, 0, keepdims=False
            )
            opening = lax.dynamic_index_in_dim(embed_rows, chosen, 0, keepdims=False)
            source = jnp.where(position == 0, opening, incoming)
            previous = lax.dynamic_index_in_dim(stored, clipped, 0, keepdims=False)
            stored = lax.dynamic_update_index_in_dim(
                stored, jnp.where(active, source, previous), clipped, 0
            )
            if counter + 1 < tick_count:
                doc_row = lax.dynamic_index_in_dim(doc_rows, chosen, 0, keepdims=False)
                sending = active & (position < sections - 1)
                result = lax.cond(
                    sending,
                    lambda: forward(source, weights, query_weight, output_weight, gain, doc_row),
                    lambda: jnp.zeros_like(source),
                )
                incoming = shifted(result, "section", 1)
        returned = jnp.zeros((length, width), jnp.bfloat16)
        normed_store = jnp.zeros((MICRO * length, width), jnp.bfloat16)
        key_store = jnp.zeros((MICRO * length, pair_width), jnp.bfloat16)
        for counter in range(tick_count):
            micro_index = counter - (sections - 1 - position)
            active = (micro_index >= 0) & (micro_index < MICRO)
            clipped = jnp.clip(micro_index, 0, MICRO - 1)
            chosen = lax.dynamic_index_in_dim(
                order, which_step * MICRO + clipped, 0, keepdims=False
            )
            target = lax.dynamic_index_in_dim(cot_rows, chosen, 0, keepdims=False)
            upstream = jnp.where(position == sections - 1, target, returned)
            kept_input = lax.dynamic_index_in_dim(stored, clipped, 0, keepdims=False)
            doc_row = lax.dynamic_index_in_dim(doc_rows, chosen, 0, keepdims=False)
            grad_input, normed_part, key_part = lax.cond(
                active,
                lambda: backward(
                    kept_input, upstream, weights, query_weight, output_weight, gain, doc_row
                ),
                lambda: (
                    jnp.zeros_like(upstream),
                    jnp.zeros((length, width), jnp.bfloat16),
                    jnp.zeros((length, pair_width), jnp.bfloat16),
                ),
            )
            row_start = clipped * length
            normed_before = lax.dynamic_slice_in_dim(normed_store, row_start, length, 0)
            key_before = lax.dynamic_slice_in_dim(key_store, row_start, length, 0)
            normed_store = lax.dynamic_update_slice_in_dim(
                normed_store, jnp.where(active, normed_part, normed_before), row_start, 0
            )
            key_store = lax.dynamic_update_slice_in_dim(
                key_store, jnp.where(active, key_part, key_before), row_start, 0
            )
            if counter + 1 < tick_count:
                returned = shifted(grad_input, "section", -1)
        return lax.dot_general(
            normed_store, key_store, (((0,), (0,)), ((), ())), preferred_element_type=jnp.float32
        )

    first_total = run_step(0, kv_stash[0])
    first_share = reduce_rows(first_total)
    second_share = reduce_rows(run_step(1, kv_now[0]))
    replicas = lax.axis_size("replica")
    grad_zero = first_share / replicas
    grad_one = second_share / replicas
    row_count = adam_m.shape[1]
    row_start = lax.axis_index("replica") * row_count
    current_rows = lax.dynamic_slice_in_dim(kv_now[0], row_start, row_count, 0)
    stash_rows, first_mid, second_mid = adam_update(current_rows, adam_m[0], adam_v[0], grad_zero)
    next_rows, moment_first, moment_second = adam_update(
        stash_rows, first_mid, second_mid, grad_one
    )
    stash_full, next_full = (
        lax.all_gather(stash_rows, "replica", axis=0, tiled=True),
        lax.all_gather(next_rows, "replica", axis=0, tiled=True),
    )
    return (stash_full[None], next_full[None], moment_first[None], moment_second[None])


def solution(mesh):
    placed = (
        P("replica", None, None, None),
        P("replica", None, None, None),
        P("replica", None),
        P("replica", None, None),
        P("section", None),
        P("section", "replica", None),
        P("section", "replica", None),
        P("section", None, None),
        P("section", None, None),
        P("section", "replica", None),
        P("section", "replica", None),
    )
    return jax.shard_map(
        body,
        mesh=mesh,
        in_specs=placed,
        out_specs=(
            P("section", None, None),
            P("section", None, None),
            P("section", "replica", None),
            P("section", "replica", None),
        ),
        check_vma=False,
    )
```

profile of v0, /device:TPU:2, one launch (start us, length us, event | category | flops | bytes accessed | tf_op | source)
XLA Modules:
  0.0 1450.1 jit_solution(17969633419464501948)
XLA Ops:
  8.8 1.7 constant_dynamic-slice_fusion.31
  27.4 76.1 %all-gather.7.cloned.1.call-done = bf16[1,2048,1024]{2,1,0:T(8,128)(2,1)} async-done(((bf16[1,32,1024]{2,1,0:T(8,128)(2,1)}), bf16[1,2048,1024]{2,1,0:T(8,128)(2,1)}) %all-gather.7.cloned.1.call-update) | async-done | bytes 4194320 | tf_op jit(solution)/shard_map/all_gather | solution.py:124
  103.5 91.0 %all-gather.5.cloned.1.call-done = bf16[1,1024,2048]{2,1,0:T(8,128)(2,1)} async-done(((bf16[1,16,2048]{2,1,0:T(8,128)(2,1)}), bf16[1,1024,2048]{2,1,0:T(8,128)(2,1)}) %all-gather.5.cloned.1.call-update) | async-done | bytes 4194320 | tf_op jit(solution)/shard_map/all_gather | solution.py:125
  194.5 8.9 conditional.18
  195.6 3.1 convolution_convert_fusion.1
  200.4 3.0 fusion
  205.7 11.3 conditional.19
  206.8 3.1 convolution_convert_fusion.4
  213.4 3.7 fusion.16
  217.0 2.3 collective-permute-start.1
  221.3 17.4 %conditional.27 = (bf16[32,2048]{1,0:T(8,128)(2,1)}) conditional(s32[]{:T(128)} %convert_element_type.1571, () %tuple.262, (bf16[1,1,32,2048]{3,2,1,0:T(8,128)(2,1)}, pred[32,2048]{1,0:T(8,128)(4,1)S(1)}, bf16[32,2048]{1,0:T(8,128)(2,1)S(1)}, bf16[2048]{0:T(1024)(128)(2,1)S(1)}, bf16[2048,512]{1,0:T(8,128)(2,1)S(1)}, ...), branch_computations={%region_46.47_spmd, %region_47.50_spmd} | conditional | flops 340874816 | bytes 13007912 | solution.py:160
  223.2 3.1 convolution_convert_fusion.32
  228.4 1.9 fusion.267
  230.3 2.0 fusion.268
  234.9 3.7 fusion.264
  238.6 1.9 collective-permute-start.8
  241.2 4.4 collective-permute-start.2
  248.3 12.1 conditional.28
  250.3 3.1 convolution_convert_fusion.35
  256.7 3.7 fusion.280
  260.4 4.7 collective-permute-start.9
  269.4 2.0 conditional.22
  272.8 9.7 collective-permute-done.4
  282.5 2.1 conditional.23
  287.6 4.3 collective-permute-done.5
  291.9 1.9 conditional.24
  296.7 125.8 %collective-permute-done.6 = bf16[32,2048]{1,0:T(8,128)(2,1)} collective-permute-done((bf16[32,2048]{1,0:T(8,128)(2,1)}, bf16[32,2048]{1,0:T(8,128)(2,1)}, u32[]{:S(2)}, u32[]{:S(2)}) %collective-permute-start.6) | collective-permute-done | bytes 131104 | tf_op jit(solution)/shard_map/ppermute | solution.py:20
  422.6 48.6 %conditional.25 = (bf16[32,2048]{1,0:T(8,128)(2,1)}, bf16[32,2048]{1,0:T(8,128)(2,1)}, bf16[32,512]{1,0:T(8,128)(2,1)}) conditional(s32[]{:T(128)} %convert_element_type.1577, () %tuple.257, (s32[1,4]{1,0:T(1,128)S(1)}, s32[]{:T(128)}, bf16[1,4,32,2048]{3,2,1,0:T(8,128)(2,1)S(1)}, pred[32,2048]{1,0:T(32,128)(4,1)S(1)}, ...), branch_computations={%region_34.35_spmd, %region_35.40_spmd} | conditional | flops 549307072 | bytes 21978450 | solution.py:180
  425.5 4.2 fusion.217
  432.5 1.7 reshape.1060
  435.6 2.1 convolution_convert_fusion.27
  441.2 3.7 convolution_convert_fusion.26
  444.9 1.7 reshape.1063
  453.1 1.9 fusion.190
  456.9 1.7 reshape.1064
  458.6 4.3 fusion.555
  466.3 2.4 fusion.197
  469.4 1.7 fusion.193
  472.4 1.7 select_dynamic-update-slice_fusion.6
  474.9 2.9 collective-permute-done.7
  477.7 23.4 %conditional.26 = (bf16[32,2048]{1,0:T(8,128)(2,1)S(1)}, bf16[32,512]{1,0:T(8,128)(2,1)S(1)}) conditional(s32[]{:T(128)} %convert_element_type.1578, () %tuple.259, (bf16[2,32,2048]{2,1,0:T(8,128)(2,1)S(1)}, s32[]{:T(128)}, bf16[2048]{0:T(1024)(128)(2,1)S(1)}, s32[1,4]{1,0:T(1,128)S(1)}, bf16[1,4,32,2048]{3,2,1,0:T(8,128)(2,1)S(1)}, ...), branch_computations={%region_40.41_spmd, %region_41.45_spmd} | conditional | flops 344850976 | bytes 31093878 | solution.py:180
  481.1 4.4 fusion.243
  487.4 2.1 convolution_convert_fusion.30
  502.8 3.7 fusion.560
  514.4 2.3 collective-permute-start.11
  521.5 6.0 collective-permute-done.12
  530.4 5.8 collective-permute-done.13
  538.9 80.3 %collective-permute-done.14 = bf16[32,2048]{1,0:T(8,128)(2,1)} collective-permute-done((bf16[32,2048]{1,0:T(8,128)(2,1)}, bf16[32,2048]{1,0:T(8,128)(2,1)}, u32[]{:S(2)}, u32[]{:S(2)}) %collective-permute-start.14) | collective-permute-done | bytes 131104 | tf_op jit(solution)/shard_map/ppermute | solution.py:20
  619.2 30.4 %conditional.34 = (bf16[32,2048]{1,0:T(8,128)(2,1)}, bf16[32,2048]{1,0:T(8,128)(2,1)S(1)}, bf16[32,512]{1,0:T(8,128)(2,1)}) conditional(s32[]{:T(128)} %convert_element_type.1577, () %tuple.275, (s32[]{:T(128)}, s32[1,4]{1,0:T(1,128)S(1)}, bf16[1,4,32,2048]{3,2,1,0:T(8,128)(2,1)S(1)}, pred[32,2048]{1,0:T(32,128)(4,1)S(1)}, ...), branch_computations={%region_80.81_spmd, %region_81.86_spmd} | conditional | flops 549307072 | bytes 23028748 | solution.py:180
  622.0 3.6 fusion.481
  629.9 3.0 convolution_convert_fusion.57
  641.0 4.3 fusion.559
  646.0 1.8 fusion.461
  647.9 1.7 fusion.457
  651.7 4.8 collective-permute-done.15
  656.5 13.3 conditional.35
  659.8 3.8 fusion.507
  664.6 1.7 convolution_convert_fusion.60
  670.8 2.7 fusion.561
  673.5 215.8 %reduce-scatter.3.cloned.1.call-done = f32[32,512]{1,0:T(8,128)} async-done(((f32[2048,512]{1,0:T(8,128)}), f32[32,512]{1,0:T(8,128)}) %reduce-scatter.3.cloned.1.call-update) | async-done | bytes 65552 | tf_op jit(solution)/shard_map/reduce_scatter | solution.py:107
  889.3 386.6 %reduce-scatter.5.cloned.1.call-done = f32[32,512]{1,0:T(8,128)} async-done(((f32[2048,512]{1,0:T(8,128)}), f32[32,512]{1,0:T(8,128)}) %reduce-scatter.5.cloned.1.call-update) | async-done | bytes 65552 | tf_op jit(solution)/shard_map/reduce_scatter | solution.py:107
  1278.2 80.0 %all-gather.11.cloned.1.call-done = bf16[2048,512]{1,0:T(8,128)(2,1)} async-done(((bf16[32,512]{1,0:T(8,128)(2,1)}), bf16[2048,512]{1,0:T(8,128)(2,1)}) %all-gather.11.cloned.1.call-update) | async-done | bytes 2097168 | tf_op jit(solution)/shard_map/all_gather | solution.py:221
  1358.2 80.2 %all-gather.9.cloned.1.call-done = bf16[2048,512]{1,0:T(8,128)(2,1)} async-done(((bf16[32,512]{1,0:T(8,128)(2,1)}), bf16[2048,512]{1,0:T(8,128)(2,1)}) %all-gather.9.cloned.1.call-update) | async-done | bytes 2097168 | tf_op jit(solution)/shard_map/all_gather | solution.py:220
  1438.5 3.0 copy.861
  (328 shorter events, 132.6 us)
Async XLA Ops:
  7.2 96.3 %all-gather.7.cloned.1.call-start = ((), (), s32[]{:S(2)}) async-start(), calls=%async_computation.3 | async-start | bytes 4259840 | tf_op jit(solution)/shard_map/all_gather | solution.py:124
  7.9 186.5 %all-gather.5.cloned.1.call-start = ((), (), s32[]{:S(2)}) async-start(), calls=%async_computation.2 | async-start | bytes 4259840 | tf_op jit(solution)/shard_map/all_gather | solution.py:125
  8.6 880.7 %reduce-scatter.3.cloned.1.call-start = ((), (), s32[]{:S(2)}) async-start(), calls=%async_computation.4 | async-start | bytes 4259840 | tf_op jit(solution)/shard_map/reduce_scatter | solution.py:107
  194.5 11.2 copy-start.9
  194.5 4.2 copy-start.3
  203.4 2.3 collective-permute-start
  205.7 15.5 %copy-start.2 = (bf16[1,2048,512]{2,1,0:T(8,128)(2,1)S(1)}, bf16[1,2048,512]{2,1,0:T(8,128)(2,1)}, u32[]{:S(2)}) copy-start(bf16[1,2048,512]{2,1,0:T(8,128)(2,1)} %param.55) | copy-start | bytes 6291460
  205.8 4.2 copy-start.4
  217.0 3.4 collective-permute-start.1
  222.3 4.4 copy-start.19
  238.6 7.1 collective-permute-start.8
  241.2 5.6 collective-permute-start.2
  248.5 5.0 copy-start.10
  260.4 9.0 copy-start.7
  260.4 9.0 copy-start.32
  260.4 6.7 collective-permute-start.9
  265.7 2.5 collective-permute-start.3
  271.4 11.2 collective-permute-start.4
  272.7 9.8 copy-start.8
  284.7 7.2 collective-permute-start.5
  293.8 128.7 %collective-permute-start.6 = (bf16[32,2048]{1,0:T(8,128)(2,1)}, bf16[32,2048]{1,0:T(8,128)(2,1)}, u32[]{:S(2)}, u32[]{:S(2)}) collective-permute-start(bf16[32,2048]{1,0:T(8,128)(2,1)} %get-tuple-element.1794), channel_id=1, source_target_pairs={{64,0},{128,64},{192,128},{65,1},{129,65},{193,129},{66,2},{130,66... | collective-permute-start | bytes 393224 | tf_op jit(solution)/shard_map/ppermute | solution.py:20
  429.9 0.6 copy-start.64
  447.8 0.7 copy-start.26
  447.8 1.8 copy-start.47
  458.6 4.3 copy-start.40
  471.1 6.6 collective-permute-start.7
  480.3 5.5 copy-start
  485.8 0.8 copy-start.17
  486.7 7.3 copy-start.43
  486.7 14.4 copy-start.18
  494.1 0.7 copy-start.31
  494.1 1.6 copy-start.52
  502.7 7.5 copy-start.73
  506.5 769.5 %reduce-scatter.5.cloned.1.call-start = ((), (), s32[]{:S(2)}) async-start(), calls=%async_computation.6 | async-start | bytes 4259840 | tf_op jit(solution)/shard_map/reduce_scatter | solution.py:107
  510.3 2.3 collective-permute-start.10
  514.4 3.5 collective-permute-start.11
  520.1 7.4 collective-permute-start.12
  529.0 7.2 collective-permute-start.13
  537.5 81.7 %collective-permute-start.14 = (bf16[32,2048]{1,0:T(8,128)(2,1)}, bf16[32,2048]{1,0:T(8,128)(2,1)}, u32[]{:S(2)}, u32[]{:S(2)}) collective-permute-start(bf16[32,2048]{1,0:T(8,128)(2,1)} %get-tuple-element.1808), channel_id=1, source_target_pairs={{64,0},{128,64},{192,128},{65,1},{129,65},{193,129},{66,2},{130,66... | collective-permute-start | bytes 393224 | tf_op jit(solution)/shard_map/ppermute | solution.py:20
  625.7 0.6 copy-start.71
  626.3 3.4 copy-start.59
  629.2 7.6 copy-start.15
  629.9 5.1 copy-start.36
  635.0 0.7 copy-start.30
  635.0 0.7 copy-start.51
  640.8 7.1 copy-start.72
  640.8 7.1 copy-start.60
  641.0 8.6 copy-start.16
  649.6 6.9 collective-permute-start.15
  659.0 5.6 copy-start.1
  670.7 605.2 %copy-start.41 = (bf16[1,32,512]{2,1,0:T(8,128)(2,1)S(1)}, bf16[1,32,512]{2,1,0:T(8,128)(2,1)}, u32[]{:S(2)}) copy-start(bf16[1,32,512]{2,1,0:T(8,128)(2,1)} %param.56) | copy-start | bytes 98308
  670.7 605.2 %copy-start.42 = (bf16[1,32,512]{2,1,0:T(8,128)(2,1)S(1)}, bf16[1,32,512]{2,1,0:T(8,128)(2,1)}, u32[]{:S(2)}) copy-start(bf16[1,32,512]{2,1,0:T(8,128)(2,1)} %param.57) | copy-start | bytes 98308
  673.5 684.7 %all-gather.11.cloned.1.call-start = ((), (), s32[]{:S(2)}) async-start(), calls=%async_computation.7 | async-start | bytes 2129920 | tf_op jit(solution)/shard_map/all_gather | solution.py:221
  1277.6 160.9 %all-gather.9.cloned.1.call-start = ((), (), s32[]{:S(2)}) async-start(), calls=%async_computation.5 | async-start | bytes 2129920 | tf_op jit(solution)/shard_map/all_gather | solution.py:220
  1358.2 83.3 %copy-start.22 = (bf16[2048,512]{1,0:T(8,128)(2,1)S(1)}, bf16[2048,512]{1,0:T(8,128)(2,1)}, u32[]{:S(2)}) copy-start(bf16[2048,512]{1,0:T(8,128)(2,1)} %all-gather.11.cloned.1.call-done) | copy-start | bytes 6291460
Sparse Core Ops, SparseCore 0:
  11.3 92.0 all-gather.6
  106.8 87.6 all-gather.4
  506.6 382.6 reduce-scatter.2
  891.8 384.0 reduce-scatter.4
  1279.7 78.5 all-gather.10
  1361.9 76.4 all-gather.8
where the time goes:
time: 1460 us; the launch traced here: 1450 us
  waiting for transfers between devices  1180 us (81%)
  matrix products  106 us (7%)
  local copies, waits for them, and re-layouts  60.1 us (4%)
  between operations  34 us (2%)
  other arithmetic  32.6 us (2%)
  starting transfers between devices  30 us (2%)
    reduce_scatter x2, waiting for transfers between devices, reduce_rows(): lax.psum_scatter(layer_total, 'replica', scatter_dimension=0, tiled=True)  602 us
    ppermute x16, waiting for transfers between devices, shifted(): return lax.ppermute(x, axis, pairs)  246 us
    all_gather x1, waiting for transfers between devices, body(): lax.all_gather(w_out, 'replica', axis=1, tiled=True)  91 us
    all_gather x1, waiting for transfers between devices, body(): lax.all_gather(stash_rows, 'replica', axis=0, tiled=True)  80.2 us
    all_gather x1, waiting for transfers between devices, body(): lax.all_gather(next_rows, 'replica', axis=0, tiled=True)  80 us
    all_gather x1, waiting for transfers between devices, body(): lax.all_gather(w_query, 'replica', axis=1, tiled=True)  76.1 us
    ppermute x16, starting transfers between devices, shifted(): return lax.ppermute(x, axis, pairs)  29.7 us
  transfers between devices with their start and end apart: 22, of which 20 were waited for; matrix products, arithmetic and copies ran while one was open for 4% of the time, Pallas kernels for 0%

commit v1 on v0

v1 whole, which is shorter than its diff:
```python
import functools

import jax
import jax.numpy as jnp
from jax import lax
from jax.experimental import pallas as pl
from jax.experimental.pallas import tpu as pltpu
from jax.sharding import PartitionSpec as P

HEAD = 64
RING = 4
REPLICAS = 64
TOKENS = 128
HALF = 64
WIDTH = 2048
QW = 1024
KVW = 512
TILE = 256
BF = jnp.bfloat16
F32 = jnp.float32
MESH = pl.DeviceIdType.MESH

beta_first = 0.9
beta_second = 0.999
learn_rate = 0.003
adam_eps = 1e-08
norm_eps = 1e-05

NN = (((1,), (0,)), ((), ()))
NT = (((1,), (1,)), ((), ()))
TN = (((0,), (0,)), ((), ()))


def mm(a, b, dims=NN):
    return lax.dot_general(a, b, dims, preferred_element_type=F32)


def wrap(v):
    return lax.rem(v + RING, RING)


class Place:
    def __init__(self):
        me = lax.axis_index("replica")
        self.z = me // 16
        self.y = lax.rem(me // 4, RING)
        self.x = lax.rem(me, RING)
        self.me = me

    def at(self, **moves):
        z = wrap(self.z + moves["z"]) if "z" in moves else self.z
        y = wrap(self.y + moves["y"]) if "y" in moves else self.y
        x = wrap(self.x + moves["x"]) if "x" in moves else self.x
        return (z * RING + y) * RING + x


class Gather:
    def __init__(self, place, parts, send, recv):
        self.place, self.parts, self.send, self.recv = place, parts, send, recv

    def chunk(self, k, src):
        ref, rows, order = self.parts[k]
        return ref.at[pl.ds(pl.multiple_of(src * rows, rows), rows), :]

    def copy(self, k, src, dst):
        piece = self.chunk(k, src)
        return pltpu.make_async_remote_copy(
            src_ref=piece,
            dst_ref=piece,
            send_sem=self.send.at[k],
            recv_sem=self.recv.at[k, src],
            device_id={"replica": dst},
            device_id_type=MESH,
        )

    def push(self, k, src, *axes):
        for axis in axes:
            for step in (1, -1):
                self.copy(k, src, self.place.at(**{axis: step})).start()

    def arrived(self, k, src):
        self.copy(k, src, self.place.at(x=1)).wait_recv()

    def begin(self):
        for k in range(len(self.parts)):
            u, v = self.parts[k][2]
            self.push(k, self.place.me, "z", u, v)

    def finish(self):
        at = self.place.at
        count = len(self.parts)
        for k in range(count):
            u, v = self.parts[k][2]
            for step in (-1, 1):
                self.arrived(k, at(z=step))
                self.push(k, at(z=step), u, v)
            off = 2 * (k % 2) - 1
            self.copy(k, at(z=off), at(z=-off)).start()
        for k in range(count):
            u, v = self.parts[k][2]
            self.arrived(k, at(z=2))
            self.push(k, at(z=2), u, v)

        def near_u(dz, carry):
            for k in range(count):
                u, v = self.parts[k][2]
                for step in (-1, 1):
                    self.arrived(k, at(**{"z": dz, u: step}))
                    self.push(k, at(**{"z": dz, u: step}), v)
                off = 2 * lax.rem(self.place.z + dz, 2) - 1
                self.copy(k, at(**{"z": dz, u: off}), at(**{u: -off})).start()
            return carry

        def far_u(dz, carry):
            for k in range(count):
                u, v = self.parts[k][2]
                self.arrived(k, at(**{"z": dz, u: 2}))
                self.push(k, at(**{"z": dz, u: 2}), v)
            return carry

        def near_v(i, carry):
            dz, du = i // RING, lax.rem(i, RING)
            for k in range(count):
                u, v = self.parts[k][2]
                for step in (-1, 1):
                    self.arrived(k, at(**{"z": dz, u: du, v: step}))
                pos_u = self.place.x if u == "x" else self.place.y
                off = 2 * lax.rem(self.place.z + dz + pos_u + du, 2) - 1
                self.copy(k, at(**{"z": dz, u: du, v: off}), at(**{v: -off})).start()
            return carry

        def far_v(i, carry):
            dz, du = i // RING, lax.rem(i, RING)
            for k in range(count):
                u, v = self.parts[k][2]
                self.arrived(k, at(**{"z": dz, u: du, v: 2}))
            return carry

        lax.fori_loop(0, RING, near_u, 0)
        lax.fori_loop(0, RING, far_u, 0)
        lax.fori_loop(0, RING * RING, near_v, 0)
        lax.fori_loop(0, RING * RING, far_v, 0)

    def drain(self):
        for k in range(len(self.parts)):
            ref, rows, order = self.parts[k]
            sent = ref.at[pl.ds(0, (REPLICAS - 1) * rows), :]
            pltpu.make_async_remote_copy(
                src_ref=sent,
                dst_ref=sent,
                send_sem=self.send.at[k],
                recv_sem=self.recv.at[k, 0],
                device_id={"replica": self.place.at(x=1)},
                device_id_type=MESH,
            ).wait_send()


class Exchange:
    def __init__(self, place, axis, out, into, send, recv):
        self.place, self.axis, self.out, self.into = place, axis, out, into
        self.send, self.recv = send, recv
        self.mine = {"x": place.x, "y": place.y, "z": place.z}[axis]

    def copies(self):
        for step in (1, 3, 2):
            there = wrap(self.mine + step)
            source = self.out(there)
            yield there, step, pltpu.make_async_remote_copy(
                src_ref=source,
                dst_ref=self.into.at[self.mine],
                send_sem=self.send.at[step - 1],
                recv_sem=self.recv.at[step - 1],
                device_id={"replica": self.place.at(**{self.axis: step})},
                device_id_type=MESH,
            )

    def start(self):
        for there, step, copy in self.copies():
            copy.start()

    def wait(self):
        for there, step, copy in self.copies():
            copy.wait_recv()
        for there, step, copy in self.copies():
            copy.wait_send()


def lower_lanes(shape):
    return lax.broadcasted_iota(jnp.int32, shape, len(shape) - 1) < HEAD


def both_halves(block, half):
    low = lower_lanes(block.shape)
    wide = block.astype(F32)
    own = jnp.where(low, wide, 0.0) if half == 0 else jnp.where(low, 0.0, wide)
    return (own + pltpu.roll(own, HEAD, 1)).astype(BF)


def head_rows(ref, group):
    blocks = []
    for j in range(4):
        start = (2 * group + j // 2) * 128
        block = ref[:, start : start + 128]
        low = lower_lanes(block.shape)
        zero = jnp.zeros_like(block)
        blocks.append(jnp.where(low, block, zero) if j % 2 == 0 else jnp.where(low, zero, block))
    return jnp.concatenate(blocks, axis=0)


def put_heads(ref, group, rows):
    low = lower_lanes((TOKENS, 128))
    for b in range(2):
        first = rows[2 * b * TOKENS : (2 * b + 1) * TOKENS]
        second = rows[(2 * b + 1) * TOKENS : (2 * b + 2) * TOKENS]
        start = (2 * group + b) * 128
        ref[:, start : start + 128] = jnp.where(low, first, second).astype(BF)


def kernel(
    emb,
    cot,
    plan,
    mask,
    gain,
    wq_share,
    wo_share,
    kv_stash,
    kv_now,
    adam_m,
    adam_v,
    stash_out,
    next_out,
    m_out,
    v_out,
    wq,
    wo,
    hid,
    up,
    fwd_out,
    bwd_out,
    normed,
    scale,
    q,
    kv,
    probs,
    mixed,
    mixed_grad,
    dq,
    dnormed,
    n_send_buf,
    n_all,
    k_all,
    x_buf,
    x_all,
    z_buf,
    z_all,
    w_send,
    w_recv,
    o_send,
    o_recv,
    hop_send,
    hop_recv,
    n_send,
    n_recv,
    k_send,
    k_recv,
    x_send,
    x_recv,
    z_send,
    z_recv,
):
    place = Place()
    section = lax.axis_index("section")
    last = RING - 1

    barrier = pltpu.get_barrier_semaphore()
    for axis in ("x", "y", "z"):
        for step in (1, 2, 3):
            pl.semaphore_signal(
                barrier, inc=1, device_id={"replica": place.at(**{axis: step})}, device_id_type=MESH
            )
    for step in (1, -1):
        pl.semaphore_signal(
            barrier, inc=1, device_id={"section": wrap(section + step)}, device_id_type=MESH
        )
    pl.semaphore_wait(barrier, 11)

    weights = Gather(place, [(wq, 32, ("x", "y")), (wo, 16, ("y", "x"))], w_send, w_recv)
    weights.chunk(0, place.me)[...] = wq_share[0]
    weights.chunk(1, place.me)[...] = wo_share[0]
    weights.begin()

    def norm_and_kv():
        def rows_of(i, carry):
            rows = pl.ds(i * 16, 16)
            wide = hid[rows, :].astype(F32)
            r = lax.rsqrt(jnp.mean(wide * wide, axis=-1, keepdims=True) + norm_eps)
            scale[rows, :] = jnp.broadcast_to(r, (16, 128))
            normed[rows, :] = (wide * r * gain[...].astype(F32)).astype(BF)
            return carry

        lax.fori_loop(0, TOKENS // 16, rows_of, 0)

        def tile(j, carry):
            cols = pl.ds(pl.multiple_of(j * TILE, TILE), TILE)
            kv[:HALF, cols] = mm(normed[:HALF, :], kv_stash[0, :, cols]).astype(BF)
            kv[HALF:, cols] = mm(normed[HALF:, :], kv_now[0, :, cols]).astype(BF)
            return carry

        lax.fori_loop(0, KVW // TILE, tile, 0)

    @pl.when(section == 0)
    def _():
        for i in range(RING):
            hid[i * 32 : (i + 1) * 32, :] = emb[0, plan[0, i]]
        norm_and_kv()

    @pl.when(section == last)
    def _():
        for i in range(RING):
            up[i * 32 : (i + 1) * 32, :] = cot[0, plan[0, i]]

    weights.finish()

    @pl.when(section > 0)
    def _():
        pltpu.make_async_remote_copy(
            src_ref=hid,
            dst_ref=hid,
            send_sem=hop_send.at[0],
            recv_sem=hop_recv.at[0],
            device_id={"section": wrap(section - 1)},
            device_id_type=MESH,
        ).wait_recv()
        norm_and_kv()

    def q_tile(j, carry):
        cols = pl.ds(pl.multiple_of(j * TILE, TILE), TILE)
        q[:, cols] = mm(normed[...], wq[:, cols]).astype(BF)
        return carry

    lax.fori_loop(0, QW // TILE, q_tile, 0)

    for group in range(4):
        start = (group // 2) * 128
        keys = both_halves(kv[:, start : start + 128], group % 2)
        values = both_halves(kv[:, 256 + start : 256 + start + 128], group % 2)
        score = mm(head_rows(q, group), keys, NT).reshape(4, TOKENS, TOKENS)
        weight = jnp.where(mask[...][None] > 0, jnp.exp(score * (HEAD**-0.5)), 0.0)
        prob = weight / jnp.sum(weight, axis=-1, keepdims=True)
        prob = prob.reshape(4 * TOKENS, TOKENS)
        probs[group] = prob

        @pl.when(section < last)
        def _():
            put_heads(mixed, group, mm(prob.astype(BF), values))

    @pl.when(section < last)
    def _():
        def out_tile(j, carry):
            cols = pl.ds(pl.multiple_of(j * TILE, TILE), TILE)
            total = hid[:, cols].astype(F32) + mm(mixed[...], wo[:, cols])
            fwd_out[:, cols] = total.astype(BF)
            pltpu.make_async_remote_copy(
                src_ref=fwd_out.at[:, cols],
                dst_ref=hid.at[:, cols],
                send_sem=hop_send.at[0],
                recv_sem=hop_recv.at[0],
                device_id={"section": wrap(section + 1)},
                device_id_type=MESH,
            ).start()
            return carry

        lax.fori_loop(0, WIDTH // TILE, out_tile, 0)

    for there in range(RING):
        for block in range(RING):
            n_send_buf[there, :, block * 128 : (block + 1) * 128] = normed[
                :, (block * RING + there) * 128 : (block * RING + there + 1) * 128
            ]
    n_trade = Exchange(place, "y", lambda there: n_send_buf.at[there], n_all, n_send, n_recv)
    n_all[place.y] = n_send_buf[place.y]
    n_trade.start()

    @pl.when(section < last)
    def _():
        pltpu.make_async_remote_copy(
            src_ref=up,
            dst_ref=up,
            send_sem=hop_send.at[1],
            recv_sem=hop_recv.at[1],
            device_id={"section": wrap(section + 1)},
            device_id_type=MESH,
        ).wait_recv()

    def mixed_tile(j, carry):
        cols = pl.ds(pl.multiple_of(j * TILE, TILE), TILE)
        mixed_grad[:, cols] = mm(up[...], wo[cols, :], NT).astype(BF)
        return carry

    lax.fori_loop(0, QW // TILE, mixed_tile, 0)

    k_mine = k_all.at[place.y]
    low = lower_lanes((TOKENS, 128))
    folded = []
    for group in range(4):
        start = (group // 2) * 128
        keys = both_halves(kv[:, start : start + 128], group % 2)
        values = both_halves(kv[:, 256 + start : 256 + start + 128], group % 2)
        heads = head_rows(q, group)
        heads_grad = head_rows(mixed_grad, group)
        prob = probs[group]
        prob_grad = mm(heads_grad, values, NT)
        inner = jnp.sum(prob_grad * prob, axis=-1, keepdims=True)
        score_grad = (prob * (prob_grad - inner) * (HEAD**-0.5)).astype(BF)
        put_heads(dq, group, mm(score_grad, keys))
        dk = mm(score_grad, heads, TN)
        dv = mm(prob.astype(BF), heads_grad, TN)
        folded.append((dk + pltpu.roll(dk, HEAD, 1), dv + pltpu.roll(dv, HEAD, 1)))
        if group % 2 == 1:
            for part in range(2):
                both = jnp.where(low, folded[group - 1][part], folded[group][part]).astype(BF)
                k_mine[:, part * 256 + start : part * 256 + start + 128] = both

    k_trade = Exchange(place, "y", lambda there: k_mine, k_all, k_send, k_recv)
    k_trade.start()

    @pl.when(section > 0)
    def _():
        def grad_tile(j, total):
            cols = pl.ds(pl.multiple_of(j * TILE, TILE), TILE)
            part = mm(dq[...], wq[cols, :], NT)
            first = mm(k_mine[:HALF, :], kv_stash[0, cols, :], NT)
            second = mm(k_mine[HALF:, :], kv_now[0, cols, :], NT)
            part = part + jnp.concatenate([first, second], axis=0)
            part = part * gain[:, cols].astype(F32)
            dnormed[:, cols] = part
            dot = part * hid[:, cols].astype(F32)
            return total + dot[:, :128] + dot[:, 128:]

        total = lax.fori_loop(0, WIDTH // TILE, grad_tile, jnp.zeros((TOKENS, 128), F32))
        r = scale[:, :1]
        inner = jnp.sum(total, axis=-1, keepdims=True) * (r * r * r) * (1.0 / WIDTH)

        def out_tile(j, carry):
            cols = pl.ds(pl.multiple_of(j * TILE, TILE), TILE)
            through = dnormed[:, cols] * r - hid[:, cols].astype(F32) * inner
            bwd_out[:, cols] = (up[:, cols].astype(F32) + through).astype(BF)
            pltpu.make_async_remote_copy(
                src_ref=bwd_out.at[:, cols],
                dst_ref=up.at[:, cols],
                send_sem=hop_send.at[1],
                recv_sem=hop_recv.at[1],
                device_id={"section": wrap(section - 1)},
                device_id_type=MESH,
            ).start()
            return carry

        lax.fori_loop(0, WIDTH // TILE, out_tile, 0)

    n_trade.wait()
    k_trade.wait()

    for step in range(2):
        tokens = slice(step * HALF, (step + 1) * HALF)
        right = k_all[:, tokens, :].reshape(RING * HALF, KVW)
        for block in range(RING):
            left = n_all[:, tokens, block * 128 : (block + 1) * 128].reshape(RING * HALF, 128)
            part = mm(left, right, TN).astype(BF)
            for there in range(RING):
                x_buf[there, block, :, step * KVW : (step + 1) * KVW] = part[
                    there * 32 : (there + 1) * 32
                ]

    x_trade = Exchange(place, "x", lambda there: x_buf.at[there], x_all, x_send, x_recv)
    x_all[place.x] = x_buf[place.x]
    x_trade.start()
    x_trade.wait()
    for block in range(RING):
        total = x_all[0, block].astype(F32)
        for there in range(1, RING):
            total = total + x_all[there, block].astype(F32)
        z_buf[block] = total.astype(BF)
    z_trade = Exchange(place, "z", lambda there: z_buf.at[there], z_all, z_send, z_recv)
    z_all[place.z] = z_buf[place.z]
    z_trade.start()
    z_trade.wait()
    grads = z_all[0].astype(F32)
    for there in range(1, RING):
        grads = grads + z_all[there].astype(F32)
    grads = grads * (1.0 / REPLICAS)

    stash_all, next_all = stash_out.at[0], next_out.at[0]
    outputs = Gather(
        place, [(stash_all, 32, ("x", "y")), (next_all, 32, ("y", "x"))], o_send, o_recv
    )
    own = pl.ds(pl.multiple_of(place.me * 32, 32), 32)
    rows = kv_now[0, own, :]
    first, second = adam_m[0], adam_v[0]
    for step, target in ((0, stash_all), (1, next_all)):
        grad = grads[:, step * KVW : (step + 1) * KVW]
        first_new = beta_first * first.astype(F32) + (1.0 - beta_first) * grad
        second_new = beta_second * second.astype(F32) + (1.0 - beta_second) * grad * grad
        moved = rows.astype(F32) - learn_rate * first_new / (jnp.sqrt(second_new) + adam_eps)
        rows, first, second = moved.astype(BF), first_new.astype(BF), second_new.astype(BF)
        target[own, :] = rows
    m_out[0] = first
    v_out[0] = second
    outputs.begin()
    outputs.finish()

    weights.drain()
    outputs.drain()

    @pl.when(section < last)
    def _():
        pltpu.make_async_remote_copy(
            src_ref=fwd_out,
            dst_ref=hid,
            send_sem=hop_send.at[0],
            recv_sem=hop_recv.at[0],
            device_id={"section": wrap(section + 1)},
            device_id_type=MESH,
        ).wait_send()

    @pl.when(section > 0)
    def _():
        pltpu.make_async_remote_copy(
            src_ref=bwd_out,
            dst_ref=up,
            send_sem=hop_send.at[1],
            recv_sem=hop_recv.at[1],
            device_id={"section": wrap(section - 1)},
            device_id_type=MESH,
        ).wait_send()


def body(
    embeddings, cotangent, plan, doc_ids, norm_gain, w_query, w_out, kv_stash, kv_now, adam_m, adam_v
):
    docs = doc_ids[0][plan[0]] + 8 * jnp.arange(4, dtype=jnp.int32)[:, None]
    docs = docs.reshape(TOKENS)
    places = jnp.arange(TOKENS)
    mask = (docs[:, None] == docs[None, :]) & (places[:, None] >= places[None, :])
    mask = mask.astype(F32)
    vmem = pl.BlockSpec(memory_space=pltpu.VMEM)
    smem = pl.BlockSpec(memory_space=pltpu.SMEM)
    dma = pltpu.SemaphoreType.DMA
    version = jax.ShapeDtypeStruct((1, WIDTH, KVW), BF)
    moment = jax.ShapeDtypeStruct((1, 32, KVW), BF)
    return pl.pallas_call(
        kernel,
        out_shape=(version, version, moment, moment),
        in_specs=[vmem, vmem, smem] + [vmem] * 8,
        out_specs=(vmem,) * 4,
        scratch_shapes=[
            pltpu.VMEM((WIDTH, QW), BF),
            pltpu.VMEM((QW, WIDTH), BF),
            pltpu.VMEM((TOKENS, WIDTH), BF),
            pltpu.VMEM((TOKENS, WIDTH), BF),
            pltpu.VMEM((TOKENS, WIDTH), BF),
            pltpu.VMEM((TOKENS, WIDTH), BF),
            pltpu.VMEM((TOKENS, WIDTH), BF),
            pltpu.VMEM((TOKENS, 128), F32),
            pltpu.VMEM((TOKENS, QW), BF),
            pltpu.VMEM((TOKENS, KVW), BF),
            pltpu.VMEM((4, 4 * TOKENS, TOKENS), F32),
            pltpu.VMEM((TOKENS, QW), BF),
            pltpu.VMEM((TOKENS, QW), BF),
            pltpu.VMEM((TOKENS, QW), BF),
            pltpu.VMEM((TOKENS, WIDTH), F32),
            pltpu.VMEM((RING, TOKENS, 512), BF),
            pltpu.VMEM((RING, TOKENS, 512), BF),
            pltpu.VMEM((RING, TOKENS, KVW), BF),
            pltpu.VMEM((RING, RING, 32, 2 * KVW), BF),
            pltpu.VMEM((RING, RING, 32, 2 * KVW), BF),
            pltpu.VMEM((RING, 32, 2 * KVW), BF),
            pltpu.VMEM((RING, 32, 2 * KVW), BF),
            dma((2,)),
            dma((2, REPLICAS)),
            dma((2,)),
            dma((2, REPLICAS)),
            dma((2,)),
            dma((2,)),
            dma((3,)),
            dma((3,)),
            dma((3,)),
            dma((3,)),
            dma((3,)),
            dma((3,)),
            dma((3,)),
            dma((3,)),
        ],
        compiler_params=pltpu.CompilerParams(
            collective_id=0, has_side_effects=True, vmem_limit_bytes=56 * 1024 * 1024
        ),
    )(embeddings, cotangent, plan, mask, norm_gain, w_query, w_out, kv_stash, kv_now, adam_m, adam_v)


def solution(mesh):
    placed = (
        P("replica", None, None, None),
        P("replica", None, None, None),
        P("replica", None),
        P("replica", None, None),
        P("section", None),
        P("section", "replica", None),
        P("section", "replica", None),
        P("section", None, None),
        P("section", None, None),
        P("section", "replica", None),
        P("section", "replica", None),
    )
    return jax.shard_map(
        body,
        mesh=mesh,
        in_specs=placed,
        out_specs=(
            P("section", None, None),
            P("section", None, None),
            P("section", "replica", None),
            P("section", "replica", None),
        ),
        check_vma=False,
    )
```

time: 1460 us -> 193 us (0.13)
  waiting for transfers between devices: 1180 us -> 0 us
  Pallas kernels: 0 us -> 184 us
  matrix products: 106 us -> 0 us
  local copies, waits for them, and re-layouts: 60.1 us -> 7.08 us
  between operations: 34 us -> 0.66 us
  other arithmetic: 32.6 us -> 1.46 us
  starting transfers between devices: 30 us -> 0 us
    reduce_scatter x2 -> x0, waiting for transfers between devices: 602 us -> none  [reduce_rows(): lax.psum_scatter(layer_total, 'replica', scatter_dimension=0, tiled=True)]
    all_gather x4 -> x0, waiting for transfers between devices: 327 us -> none  [the longest x1 91 us: body(): lax.all_gather(w_out, 'replica', axis=1, tiled=True)]
    ppermute x16 -> x0, waiting for transfers between devices: 246 us -> none  [shifted(): return lax.ppermute(x, axis, pairs)]
    pallas_call x0 -> x1, Pallas kernels: none -> 184 us  [body(): pl.pallas_call(kernel, out_shape=(version, version, moment, moment), in_s...]
    dot_general x56 -> x0, matrix products: 106 us -> none  [the longest x8 21.7 us: project_in(): jnp.dot(normed, query_weight, preferred_element_type=jnp.float32)]
    ppermute x16 -> x0, starting transfers between devices: 29.7 us -> none  [shifted(): return lax.ppermute(x, axis, pairs)]
    reshape x38 -> x0, local copies, waits for them, and re-layouts: 20.9 us -> none  [the longest x10 6.51 us: attend_core(): queries.reshape(length, kv_heads, -1, HEAD).astype(jnp.float32)]
    dynamic_update_slice x27 -> x0, other arithmetic: 14.9 us -> none  [the longest x10 7.59 us: run_step(): lax.dynamic_update_slice_in_dim(normed_store, jnp.where(active, normed_pa...]
  transfers between devices with their start and end apart: 22 -> 0, of which waited for: 20 -> 0; matrix products, arithmetic and copies ran while one was open for 4% -> 0% of each run, Pallas kernels for 0% -> 0%
where the time goes in v1:
time: 193 us
  Pallas kernels  184 us (95%)
  local copies, waits for them, and re-layouts  7.08 us (4%)
    pallas_call x1, Pallas kernels, body(): pl.pallas_call(kernel, out_shape=(version, version, moment, moment), in_s...  184 us
    unnamed x12, local copies, waits for them, and re-layouts  6.43 us

profile of v1, /device:TPU:2, one launch (start us, length us, event | category | flops | bytes accessed | tf_op | source)
XLA Modules:
  0.0 192.8 jit_solution(11945346254541972824)
XLA Ops:
  0.6 0.0 copy-start
  0.6 0.7 copy-done
  1.3 0.7 fusion.2
  2.0 0.6 gather_fusion
  2.5 0.1 broadcast_add_fusion
  2.6 0.1 add.32
  2.7 0.7 fusion.1.mask
  3.4 183.6 %shard_map.138 = (bf16[1,2048,512]{2,1,0:T(8,128)(2,1)}, bf16[1,2048,512]{2,1,0:T(8,128)(2,1)}, bf16[1,32,512]{2,1,0:T(8,128)(2,1)}, bf16[1,32,512]{2,1,0:T(8,128)(2,1)}) custom-call(bf16[1,4,32,2048]{3,2,1,0:T(8,128)(2,1)} %emb.1, bf16[1,4,32,2048]{3,2,1,0:T(8,128)(2,1)} %cot.1, s32[1,4]{1,0:T(1,128)} %plan.1, f32[128,128]{1,0:T(8,128)} %fusion.1.mask, ...), custom_call_target="tpu_custom_call" | custom-call | tf_op jit(solution)/shard_map/pallas_call | solution.py:551
  187.0 0.0 copy-start.1
  187.0 3.2 %copy.19 = bf16[1,2048,512]{2,1,0:T(8,128)(2,1)} copy(bf16[1,2048,512]{2,1,0:T(8,128)(2,1)} %get-tuple-element.8) | data formatting | bytes 4194304
  190.2 0.0 copy-done.1
  190.2 0.0 copy-start.3
  190.2 0.0 copy-start.2
  190.2 1.3 copy.20
  191.5 0.0 copy-done.3
  191.5 0.6 copy.21
  192.1 0.0 copy-done.2
  192.1 0.6 copy.22
  (2 shorter events, 0.0 us)
Async XLA Ops:
  0.6 0.7 copy-start
  187.0 3.2 %copy-start.1 = (bf16[1,2048,512]{2,1,0:T(8,128)(2,1)S(1)}, bf16[1,2048,512]{2,1,0:T(8,128)(2,1)}, u32[]{:S(2)}) copy-start(bf16[1,2048,512]{2,1,0:T(8,128)(2,1)} %get-tuple-element.9) | copy-start | bytes 6291460
  190.2 1.3 copy-start.3
  190.2 1.9 %copy-start.2 = (bf16[1,32,512]{2,1,0:T(8,128)(2,1)S(1)}, bf16[1,32,512]{2,1,0:T(8,128)(2,1)}, u32[]{:S(2)}) copy-start(bf16[1,32,512]{2,1,0:T(8,128)(2,1)} %get-tuple-element.11) | copy-start | bytes 98308

commit v2 on v1

v2 whole, which is shorter than its diff:
```python
import functools

import jax
import jax.numpy as jnp
from jax import lax
from jax.experimental import pallas as pl
from jax.experimental.pallas import tpu as pltpu
from jax.sharding import PartitionSpec as P

HEAD = 64
RING = 4
REPLICAS = 64
TOKENS = 128
HALF = 64
WIDTH = 2048
QW = 1024
KVW = 512
WIDE = 512
CHUNKS = 4
BF = jnp.bfloat16
F32 = jnp.float32
MESH = pl.DeviceIdType.MESH

beta_first = 0.9
beta_second = 0.999
learn_rate = 0.003
adam_eps = 1e-08
norm_eps = 1e-05

NN = (((1,), (0,)), ((), ()))
NT = (((1,), (1,)), ((), ()))
TN = (((0,), (0,)), ((), ()))


def mm(a, b, dims=NN):
    return lax.dot_general(a, b, dims, preferred_element_type=F32)


def wrap(v):
    return lax.rem(v + RING, RING)


class Place:
    def __init__(self):
        me = lax.axis_index("replica")
        self.me = me
        self.z = me // 16
        self.y = lax.rem(me // 4, RING)
        self.x = lax.rem(me, RING)
        self.line = {}
        for axis, own in (("z", self.z), ("y", self.y), ("x", self.x)):
            self.line[axis] = [own] + [wrap(own + step) for step in range(1, RING)]

    def on(self, axis, step):
        return self.line[axis][step % RING]

    def at(self, axis, step):
        spot = {"z": self.z, "y": self.y, "x": self.x}
        spot[axis] = self.on(axis, step)
        return (spot["z"] * RING + spot["y"]) * RING + spot["x"]


class Gather:
    def __init__(self, place, parts, send, recv, direct, far):
        self.place, self.parts, self.send, self.recv = place, parts, send, recv
        self.direct, self.far = direct, far
        self.peer = {
            (axis, step): place.at(axis, step) for axis in ("x", "y", "z") for step in (1, -1, 2)
        }

    def piece(self, k, dz, du=0, dv=0, many=None):
        ref, first, columns, u, v = self.parts[k]
        spot = {u: self.place.on(u, du), v: self.place.on(v, dv)}
        if many is not None:
            spot[u] = many
        return ref.at[self.place.on("z", dz), spot["y"], spot["x"], :, pl.ds(first, columns)]

    def copy(self, k, piece, axis, step, slot):
        stage = 0 if slot < 3 else 1 if slot < 15 else 2
        return pltpu.make_async_remote_copy(
            src_ref=piece,
            dst_ref=piece,
            send_sem=self.send.at[k, stage],
            recv_sem=self.recv.at[k, slot],
            device_id={"replica": self.peer[axis, step]},
            device_id_type=MESH,
        )

    def along_z(self, k, start):
        for step in (1, -1):
            copy = self.copy(k, self.piece(k, 0 if start else -step), "z", step, (1 - step) // 2)
            copy.start() if start else copy.wait_recv()

    def past_z(self, k, start):
        step = 1 if k % 2 else -1
        source = -step
        if self.far:
            step, source = 2, 0
        copy = self.copy(k, self.piece(k, source if start else 2), "z", step, 2)
        copy.start() if start else copy.wait_recv()

    def along_u(self, k, dz, start):
        u = self.parts[k][3]
        for step in (1, -1):
            piece = self.piece(k, dz, 0 if start else -step)
            copy = self.copy(k, piece, u, step, 3 + 3 * (dz % RING) + (1 - step) // 2)
            copy.start() if start else copy.wait_recv()

    def past_u(self, k, dz, start):
        u = self.parts[k][3]
        step = 1 if dz % 2 else -1
        source = -step
        if dz % RING in self.direct:
            step, source = 2, 0
        piece = self.piece(k, dz, source if start else 2)
        copy = self.copy(k, piece, u, step, 3 + 3 * (dz % RING) + 2)
        copy.start() if start else copy.wait_recv()

    def along_v(self, k, dz, start):
        v = self.parts[k][4]
        for step in (1, -1):
            piece = self.piece(k, dz, 0, 0 if start else -step, slice(0, RING))
            copy = self.copy(k, piece, v, step, 15 + 4 * (dz % RING) + (1 - step) // 2)
            copy.start() if start else copy.wait_recv()

    def past_v(self, k, dz, start):
        v = self.parts[k][4]
        for step in (1, -1):
            half = slice(0, 2) if step == 1 else slice(2, RING)
            piece = self.piece(k, dz, 0, -step if start else 2, half)
            copy = self.copy(k, piece, v, step, 17 + 4 * (dz % RING) + (1 - step) // 2)
            copy.start() if start else copy.wait_recv()

    def send_u(self, k, dz):
        self.along_u(k, dz, True)
        if dz % RING in self.direct:
            self.past_u(k, dz, True)

    def take_u(self, k, dz):
        self.along_u(k, dz, False)
        if dz % RING not in self.direct:
            self.past_u(k, dz, True)

    def send_v(self, k, dz):
        self.past_u(k, dz, False)
        self.along_v(k, dz, True)

    def take_v(self, k, dz):
        self.along_v(k, dz, False)
        self.past_v(k, dz, True)

    def begin(self, parts):
        for k in parts:
            self.along_z(k, True)
        for k in parts:
            self.send_u(k, 0)
        for k in parts:
            if self.far:
                self.past_z(k, True)

    def finish(self, parts):
        def each(step, *planes):
            for dz in planes:
                for k in parts:
                    step(k, dz)

        each(self.take_u, 0)
        each(self.send_v, 0)
        for k in parts:
            self.along_z(k, False)
            if not self.far:
                self.past_z(k, True)
        each(self.send_u, -1, 1)
        each(self.take_u, -1, 1)
        each(self.take_v, 0)
        for k in parts:
            self.past_z(k, False)
        each(self.send_u, 2)
        each(self.send_v, -1, 1)
        each(self.take_u, 2)
        each(self.send_v, 2)
        each(self.take_v, -1, 1, 2)
        each(lambda k, dz: self.past_v(k, dz, False), 0, -1, 1, 2)

    def drain(self):
        for k in range(len(self.parts)):
            ref, first, columns = self.parts[k][:3]
            columns = pl.ds(first, columns)
            sent = (
                ref.at[0, 0, 0:3, :, columns],
                ref.at[0, 0:3, :, :, columns],
                ref.at[0:3, :, :, :, columns],
            )
            for piece, slot in zip(sent, (0, 3, 15)):
                self.copy(k, piece, "x", 1, slot).wait_send()


class Exchange:
    def __init__(self, place, axis, out, into, send, recv):
        self.place, self.axis, self.out, self.into = place, axis, out, into
        self.send, self.recv = send, recv
        self.mine = {"x": place.x, "y": place.y, "z": place.z}[axis]

    def copies(self):
        for step in (1, 3, 2):
            there = self.place.on(self.axis, step)
            source = self.out(there)
            yield there, step, pltpu.make_async_remote_copy(
                src_ref=source,
                dst_ref=self.into.at[self.mine],
                send_sem=self.send.at[step - 1],
                recv_sem=self.recv.at[step - 1],
                device_id={"replica": self.place.at(self.axis, step)},
                device_id_type=MESH,
            )

    def start(self):
        for there, step, copy in self.copies():
            copy.start()

    def wait(self):
        for there, step, copy in self.copies():
            copy.wait_recv()
        for there, step, copy in self.copies():
            copy.wait_send()


def lower_lanes(shape):
    return lax.broadcasted_iota(jnp.int32, shape, len(shape) - 1) < HEAD


def both_halves(block, half):
    low = lower_lanes(block.shape)
    wide = block.astype(F32)
    own = jnp.where(low, wide, 0.0) if half == 0 else jnp.where(low, 0.0, wide)
    return (own + pltpu.roll(own, HEAD, 1)).astype(BF)


def head_rows(ref, group):
    blocks = []
    for j in range(4):
        start = (2 * group + j // 2) * 128
        block = ref[:, start : start + 128]
        low = lower_lanes(block.shape)
        zero = jnp.zeros_like(block)
        blocks.append(jnp.where(low, block, zero) if j % 2 == 0 else jnp.where(low, zero, block))
    return jnp.concatenate(blocks, axis=0)


def put_heads(ref, group, rows):
    low = lower_lanes((TOKENS, 128))
    for b in range(2):
        first = rows[2 * b * TOKENS : (2 * b + 1) * TOKENS]
        second = rows[(2 * b + 1) * TOKENS : (2 * b + 2) * TOKENS]
        start = (2 * group + b) * 128
        ref[:, start : start + 128] = jnp.where(low, first, second).astype(BF)


def kernel(
    emb_in,
    cot_in,
    plan,
    docs,
    gain,
    wq_share,
    wo_share,
    stash_in,
    now_in,
    adam_m,
    adam_v,
    stash_out,
    next_out,
    m_out,
    v_out,
    emb,
    cot,
    kv_stash,
    kv_now,
    tags,
    wq,
    wo,
    wq_t,
    wo_t,
    stash_t,
    now_t,
    hid,
    up,
    fwd_out,
    bwd_out,
    wide,
    scale,
    q,
    kv,
    probs,
    mixed,
    mixed_grad,
    dq,
    kg,
    n_t,
    n_y,
    n_x,
    k_y,
    k_x,
    x_buf,
    x_all,
    y_buf,
    y_all,
    z_buf,
    z_all,
    w_send,
    w_recv,
    o_send,
    o_recv,
    hop_send,
    hop_recv,
    trade_send,
    trade_recv,
    load_sem,
):
    place = Place()
    section = lax.axis_index("section")
    last = RING - 1

    loads = [
        pltpu.make_async_copy(src, dst, load_sem.at[i])
        for i, (src, dst) in enumerate(
            ((emb_in, emb), (cot_in, cot), (stash_in, kv_stash), (now_in, kv_now))
        )
    ]
    for load in loads:
        load.start()

    def load_wait():
        for load in loads:
            load.wait()

    barrier = pltpu.get_barrier_semaphore()
    for axis in ("x", "y", "z"):
        for step in (1, 2, 3):
            pl.semaphore_signal(
                barrier, inc=1, device_id={"replica": place.at(axis, step)}, device_id_type=MESH
            )
    for step in (1, -1):
        pl.semaphore_signal(
            barrier, inc=1, device_id={"section": wrap(section + step)}, device_id_type=MESH
        )
    pl.semaphore_wait(barrier, 11)

    def columns(c, size=WIDE):
        return slice(c * size, (c + 1) * size)

    def hop(way, src, dst, c, to):
        return pltpu.make_async_remote_copy(
            src_ref=src.at[:, columns(c)],
            dst_ref=dst.at[:, columns(c)],
            send_sem=hop_send.at[way, c],
            recv_sem=hop_recv.at[way, c],
            device_id={"section": wrap(section + to)},
            device_id_type=MESH,
        )

    def drain_hops():
        @pl.when(section < last)
        def _():
            for c in range(CHUNKS):
                hop(0, fwd_out, hid, c, 1).wait_send()

        @pl.when(section > 0)
        def _():
            for c in range(CHUNKS):
                hop(1, bwd_out, up, c, -1).wait_send()

    def four(block):
        return block[:, :128] + block[:, 128:256] + block[:, 256:384] + block[:, 384:]

    def allowed():
        tag = jnp.broadcast_to(tags[:1, :], (TOKENS, TOKENS))
        row = lax.broadcasted_iota(jnp.int32, (TOKENS, TOKENS), 0)
        col = lax.broadcasted_iota(jnp.int32, (TOKENS, TOKENS), 1)
        return (tag == tag.T) & (row // 32 == col // 32) & (row >= col)

    def project():
        @pl.when(section == 0)
        def _():
            for i in range(RING):
                hid[i * 32 : (i + 1) * 32, :] = emb[0, plan[0, i]]

        for c in range(CHUNKS):
            cols = columns(c)

            @pl.when(section > 0)
            def _():
                hop(0, fwd_out, hid, c, -1).wait_recv()

            own = hid[:, cols].astype(F32)
            gained = (own * gain[:, cols].astype(F32)).astype(BF)
            squares = four(own * own)
            products = (
                mm(gained, wq[c].reshape(WIDE, QW)),
                mm(gained[:HALF], kv_stash[0, cols, :]),
                mm(gained[HALF:], kv_now[0, cols, :]),
            )
            if c == 0:
                wide[:, :QW] = products[0]
                wide[:HALF, QW : QW + KVW] = products[1]
                wide[HALF:, QW : QW + KVW] = products[2]
                scale[...] = squares
            else:
                wide[:, :QW] += products[0]
                wide[:HALF, QW : QW + KVW] += products[1]
                wide[HALF:, QW : QW + KVW] += products[2]
                scale[...] += squares
        mean = jnp.sum(scale[...], axis=-1, keepdims=True) * (1.0 / WIDTH)
        r = lax.rsqrt(mean + norm_eps)
        scale[...] = jnp.broadcast_to(r, (TOKENS, 128))
        q[...] = (wide[:, :QW] * r).astype(BF)
        kv[...] = (wide[:, QW : QW + KVW] * r).astype(BF)

        mask = allowed()
        for group in range(4):
            start = (group // 2) * 128
            keys = both_halves(kv[:, start : start + 128], group % 2)
            values = both_halves(kv[:, 256 + start : 256 + start + 128], group % 2)
            score = mm(head_rows(q, group), keys, NT).reshape(4, TOKENS, TOKENS)
            weight = jnp.where(mask[None], jnp.exp(score * (HEAD**-0.5)), 0.0)
            prob = weight / jnp.sum(weight, axis=-1, keepdims=True)
            prob = prob.reshape(4 * TOKENS, TOKENS)
            probs[group] = prob

            @pl.when(section < last)
            def _():
                put_heads(mixed, group, mm(prob.astype(BF), values))

    def prepare():
        def turn(i, carry):
            rows = pl.ds(pl.multiple_of(i * WIDE, WIDE), WIDE)
            wq_t[:, rows] = wq[i].reshape(WIDE, QW).T
            stash_t[:, rows] = kv_stash[0, rows, :].T
            now_t[:, rows] = kv_now[0, rows, :].T
            return carry

        def turn_out(i, carry):
            rows = pl.ds(pl.multiple_of(i * 256, 256), 256)
            wo_t[:, rows] = wo[i].reshape(256, WIDTH).T
            return carry

        lax.fori_loop(0, RING, turn_out, 0)
        lax.fori_loop(0, RING, turn, 0)

    def trade(index, axis, out, into):
        return Exchange(place, axis, out, into, trade_send.at[index], trade_recv.at[index])

    n_trades = (
        trade(0, "y", lambda there: n_t.at[0:2, there], n_y),
        trade(1, "x", lambda there: n_t.at[2:4, :, there], n_x),
    )
    k_trades = (trade(2, "y", lambda there: kg, k_y), trade(3, "x", lambda there: kg, k_x))

    def share_normed():
        for block in range(RING * RING):
            cols = columns(block, 128)
            own = hid[:, cols].astype(F32) * scale[...] * gain[:, cols].astype(F32)
            n_t[block // RING, block % RING] = own.astype(BF).T.reshape(RING, 32, TOKENS)
        n_y[place.y] = n_t[0:2, place.y]
        n_x[place.x] = n_t[2:4, :, place.x]
        for one in n_trades:
            one.start()

    def make_mixed_grad(streamed):
        for c in range(CHUNKS):
            if streamed:
                hop(1, bwd_out, up, c, 1).wait_recv()
            part = mm(up[:, columns(c)], wo_t[columns(c), :])
            if c == 0:
                wide[:, :QW] = part
            elif c < CHUNKS - 1:
                wide[:, :QW] += part
            else:
                mixed_grad[...] = (wide[:, :QW] + part).astype(BF)

    weights = Gather(
        place,
        [
            (wq, 0, QW // 2, "x", "y"),
            (wq, QW // 2, QW // 2, "y", "x"),
            (wo, 0, WIDTH // 2, "x", "y"),
            (wo, WIDTH // 2, WIDTH // 2, "y", "x"),
        ],
        w_send,
        w_recv,
        (),
        False,
    )
    wq[place.z, place.y, place.x] = wq_share[0]
    wo[place.z, place.y, place.x] = wo_share[0]

    weights.begin((0, 1, 2, 3))
    for i in range(RING):
        tags[:1, i * 32 : (i + 1) * 32] = docs[0, pl.ds(plan[0, i], 1), :].astype(F32)
    weights.finish((0, 1, 2, 3))

    load_wait()

    @pl.when(section == last)
    def _():
        prepare()
        for i in range(RING):
            up[i * 32 : (i + 1) * 32, :] = cot[0, plan[0, i]]
        make_mixed_grad(False)

    project()

    @pl.when(section < last)
    def _():
        for c in range(CHUNKS):
            cols = columns(c)
            fwd_out[:, cols] = (hid[:, cols].astype(F32) + mm(mixed[...], wo[:, :, :, :, cols].reshape(QW, WIDE))).astype(BF)
            hop(0, fwd_out, hid, c, 1).start()
        prepare()
        share_normed()
        make_mixed_grad(True)

    low = lower_lanes((TOKENS, 128))
    folded = []
    for group in range(4):
        start = (group // 2) * 128
        keys = both_halves(kv[:, start : start + 128], group % 2)
        values = both_halves(kv[:, 256 + start : 256 + start + 128], group % 2)
        heads = head_rows(q, group)
        heads_grad = head_rows(mixed_grad, group)
        prob = probs[group]
        prob_grad = mm(heads_grad, values, NT)
        inner = jnp.sum(prob_grad * prob, axis=-1, keepdims=True)
        score_grad = (prob * (prob_grad - inner) * (HEAD**-0.5)).astype(BF)
        put_heads(dq, group, mm(score_grad, keys))
        dk = mm(score_grad, heads, TN)
        dv = mm(prob.astype(BF), heads_grad, TN)
        folded.append((dk + pltpu.roll(dk, HEAD, 1), dv + pltpu.roll(dv, HEAD, 1)))
        if group % 2 == 1:
            for part in range(2):
                both = jnp.where(low, folded[group - 1][part], folded[group][part]).astype(BF)
                kg[:, part * 256 + start : part * 256 + start + 128] = both

    k_y[place.y] = kg[...]
    k_x[place.x] = kg[...]
    for one in k_trades:
        one.start()

    @pl.when(section > 0)
    def _():
        total = jnp.zeros((TOKENS, 128), F32)
        for c in range(CHUNKS):
            cols = columns(c)
            first = mm(kg[:HALF, :], stash_t[:, cols])
            second = mm(kg[HALF:, :], now_t[:, cols])
            part = mm(dq[...], wq_t[:, cols]) + jnp.concatenate([first, second], axis=0)
            part = part * gain[:, cols].astype(F32)
            wide[:, cols] = part
            total = total + four(part * hid[:, cols].astype(F32))
        r = scale[...]
        inner = jnp.sum(total, axis=-1, keepdims=True) * (1.0 / WIDTH)
        inner = jnp.broadcast_to(inner, (TOKENS, 128)) * (r * r * r)
        for c in range(CHUNKS):
            for d in range(RING):
                cols = columns(c * RING + d, 128)
                through = wide[:, cols] * r - hid[:, cols].astype(F32) * inner
                bwd_out[:, cols] = (up[:, cols].astype(F32) + through).astype(BF)
            hop(1, bwd_out, up, c, -1).start()

    @pl.when(section == last)
    def _():
        share_normed()

    for one in n_trades + k_trades:
        one.wait()
    token = lax.broadcasted_iota(jnp.int32, (256, RING * TOKENS), 1)
    early = lax.rem(token, TOKENS) < HALF
    for n_all, k_all, buf in ((n_y, k_y, x_buf), (n_x, k_x, y_buf)):
        left = jnp.concatenate([n_all[src].reshape(256, TOKENS) for src in range(RING)], axis=1)
        right = k_all[...].reshape(RING * TOKENS, KVW)
        zero = jnp.zeros_like(left)
        for step in range(2):
            own = jnp.where(early, left, zero) if step == 0 else jnp.where(early, zero, left)
            part = mm(own, right).astype(BF).reshape(2, RING, 32, KVW)
            for there in range(RING):
                buf[there, :, :, step * KVW : (step + 1) * KVW] = part[:, there]
        one = (
            trade(4, "x", lambda there: x_buf.at[there], x_all)
            if buf is x_buf
            else trade(5, "y", lambda there: y_buf.at[there], y_all)
        )
        one.start()
    x_all[place.x] = x_buf[place.x]
    y_all[place.y] = y_buf[place.y]
    trade(4, "x", lambda there: x_buf.at[there], x_all).wait()
    trade(5, "y", lambda there: y_buf.at[there], y_all).wait()
    for start, parts in ((0, x_all), (2, y_all)):
        total = parts[0].astype(F32)
        for src in range(1, RING):
            total = total + parts[src].astype(F32)
        z_buf[start : start + 2] = total.astype(BF)
    z_trade = trade(6, "z", lambda there: z_buf.at[there], z_all)
    z_all[place.z] = z_buf[place.z]
    z_trade.start()
    z_trade.wait()
    grads = z_all[0].astype(F32)
    for src in range(1, RING):
        grads = grads + z_all[src].astype(F32)
    grads = grads * (1.0 / REPLICAS)
    outputs = Gather(
        place, [(stash_out, 0, KVW, "x", "y"), (next_out, 0, KVW, "y", "x")], o_send, o_recv, (0, 1, 2, 3), True
    )
    own = pl.ds(pl.multiple_of(place.me * 32, 32), 32)
    rows = kv_now[0, own, :]
    first, second = adam_m[0], adam_v[0]
    for step, target in ((0, stash_out), (1, next_out)):
        grad = grads[:, step * KVW : (step + 1) * KVW]
        first_new = beta_first * first.astype(F32) + (1.0 - beta_first) * grad
        second_new = beta_second * second.astype(F32) + (1.0 - beta_second) * grad * grad
        moved = rows.astype(F32) - learn_rate * first_new / (jnp.sqrt(second_new) + adam_eps)
        rows, first, second = moved.astype(BF), first_new.astype(BF), second_new.astype(BF)
        target[place.z, place.y, place.x] = rows
        outputs.begin((step,))
    m_out[0] = first
    v_out[0] = second
    outputs.finish((0, 1))

    weights.drain()
    outputs.drain()
    drain_hops()


def body(
    embeddings, cotangent, plan, doc_ids, norm_gain, w_query, w_out, kv_stash, kv_now, adam_m, adam_v
):
    vmem = pl.BlockSpec(memory_space=pltpu.VMEM)
    smem = pl.BlockSpec(memory_space=pltpu.SMEM)
    hbm = pl.BlockSpec(memory_space=pl.ANY)
    dma = pltpu.SemaphoreType.DMA
    version = jax.ShapeDtypeStruct((RING, RING, RING, 32, KVW), BF)
    moment = jax.ShapeDtypeStruct((1, 32, KVW), BF)
    stash, current, first, second = pl.pallas_call(
        kernel,
        out_shape=(version, version, moment, moment),
        in_specs=[hbm, hbm, smem, vmem, vmem, vmem, vmem, hbm, hbm, vmem, vmem],
        out_specs=(vmem,) * 4,
        scratch_shapes=[
            pltpu.VMEM((1, 4, 32, WIDTH), BF),
            pltpu.VMEM((1, 4, 32, WIDTH), BF),
            pltpu.VMEM((1, WIDTH, KVW), BF),
            pltpu.VMEM((1, WIDTH, KVW), BF),
            pltpu.VMEM((8, TOKENS), F32),
            pltpu.VMEM((RING, RING, RING, 32, QW), BF),
            pltpu.VMEM((RING, RING, RING, 16, WIDTH), BF),
            pltpu.VMEM((QW, WIDTH), BF),
            pltpu.VMEM((WIDTH, QW), BF),
            pltpu.VMEM((KVW, WIDTH), BF),
            pltpu.VMEM((KVW, WIDTH), BF),
            pltpu.VMEM((TOKENS, WIDTH), BF),
            pltpu.VMEM((TOKENS, WIDTH), BF),
            pltpu.VMEM((TOKENS, WIDTH), BF),
            pltpu.VMEM((TOKENS, WIDTH), BF),
            pltpu.VMEM((TOKENS, WIDTH), F32),
            pltpu.VMEM((TOKENS, 128), F32),
            pltpu.VMEM((TOKENS, QW), BF),
            pltpu.VMEM((TOKENS, KVW), BF),
            pltpu.VMEM((4, 4 * TOKENS, TOKENS), F32),
            pltpu.VMEM((TOKENS, QW), BF),
            pltpu.VMEM((TOKENS, QW), BF),
            pltpu.VMEM((TOKENS, QW), BF),
            pltpu.VMEM((TOKENS, KVW), BF),
            pltpu.VMEM((RING, RING, RING, 32, TOKENS), BF),
            pltpu.VMEM((RING, 2, RING, 32, TOKENS), BF),
            pltpu.VMEM((RING, 2, RING, 32, TOKENS), BF),
            pltpu.VMEM((RING, TOKENS, KVW), BF),
            pltpu.VMEM((RING, TOKENS, KVW), BF),
            pltpu.VMEM((RING, 2, 32, 2 * KVW), BF),
            pltpu.VMEM((RING, 2, 32, 2 * KVW), BF),
            pltpu.VMEM((RING, 2, 32, 2 * KVW), BF),
            pltpu.VMEM((RING, 2, 32, 2 * KVW), BF),
            pltpu.VMEM((RING, 32, 2 * KVW), BF),
            pltpu.VMEM((RING, 32, 2 * KVW), BF),
            dma((4, 3)),
            dma((4, 31)),
            dma((2, 3)),
            dma((2, 31)),
            dma((2, CHUNKS)),
            dma((2, CHUNKS)),
            dma((7, RING - 1)),
            dma((7, RING - 1)),
            dma((4,)),
        ],
        compiler_params=pltpu.CompilerParams(
            collective_id=0, has_side_effects=True, vmem_limit_bytes=56 * 1024 * 1024
        ),
    )(embeddings, cotangent, plan, doc_ids, norm_gain, w_query, w_out, kv_stash, kv_now, adam_m, adam_v)
    shape = (1, WIDTH, KVW)
    return stash.reshape(shape), current.reshape(shape), first, second


def solution(mesh):
    placed = (
        P("replica", None, None, None),
        P("replica", None, None, None),
        P("replica", None),
        P("replica", None, None),
        P("section", None),
        P("section", "replica", None),
        P("section", "replica", None),
        P("section", None, None),
        P("section", None, None),
        P("section", "replica", None),
        P("section", "replica", None),
    )
    return jax.shard_map(
        body,
        mesh=mesh,
        in_specs=placed,
        out_specs=(
            P("section", None, None),
            P("section", None, None),
            P("section", "replica", None),
            P("section", "replica", None),
        ),
        check_vma=False,
    )
```

time: 193 us -> 165 us (0.85)
  Pallas kernels: 184 us -> 158 us
    pallas_call x1, Pallas kernels: 184 us -> 158 us  [body(): pl.pallas_call(kernel, out_shape=(version, version, moment, moment), in_s...]
    unnamed x12 -> x10, local copies, waits for them, and re-layouts: 6.43 us -> 5.75 us
where the time goes in v2:
time: 165 us
  Pallas kernels  158 us (96%)
  local copies, waits for them, and re-layouts  5.75 us (3%)
    pallas_call x1, Pallas kernels, body(): pl.pallas_call(kernel, out_shape=(version, version, moment, moment), in_s...  158 us
    unnamed x10, local copies, waits for them, and re-layouts  5.75 us

profile of v2, /device:TPU:2, one launch (start us, length us, event | category | flops | bytes accessed | tf_op | source)
XLA Modules:
  0.0 164.9 jit_solution(3761859697759771527)
XLA Ops:
  0.6 158.5 %shard_map.138 = (bf16[4,4,4,32,512]{4,3,2,1,0:T(8,128)(2,1)}, bf16[4,4,4,32,512]{4,3,2,1,0:T(8,128)(2,1)}, bf16[1,32,512]{2,1,0:T(8,128)(2,1)}, bf16[1,32,512]{2,1,0:T(8,128)(2,1)}) custom-call(bf16[1,4,32,2048]{3,2,1,0:T(8,128)(2,1)} %emb_in.1, bf16[1,4,32,2048]{3,2,1,0:T(8,128)(2,1)} %cot_in.1, s32[1,4]{1,0:T(1,128)} %plan.1, s32[1,4,32]{2,1,0:T(4,128)} %docs.1, ...), custom_call_target="tpu_custom_call" | custom-call | tf_op jit(solution)/shard_map/pallas_call | solution.py:642
  159.1 0.0 copy-start
  159.1 3.2 %copy.19 = bf16[1,2048,512]{2,1,0:T(8,128)(2,1)} copy(bf16[1,2048,512]{2,1,0:T(8,128)(2,1)} %bitcast.3) | data formatting | bytes 4194304
  162.3 0.0 copy-done
  162.3 0.0 copy-start.2
  162.3 0.0 copy-start.1
  162.3 1.3 copy.20
  163.7 0.0 copy-done.2
  163.7 0.6 copy.21
  164.3 0.0 copy-done.1
  164.3 0.6 copy.22
Async XLA Ops:
  159.1 3.2 %copy-start = (bf16[4,4,4,32,512]{4,3,2,1,0:T(8,128)(2,1)S(1)}, bf16[4,4,4,32,512]{4,3,2,1,0:T(8,128)(2,1)}, u32[]{:S(2)}) copy-start(bf16[4,4,4,32,512]{4,3,2,1,0:T(8,128)(2,1)} %get-tuple-element.9) | copy-start | bytes 6291460
  162.3 1.3 copy-start.2
  162.3 1.9 %copy-start.1 = (bf16[1,32,512]{2,1,0:T(8,128)(2,1)S(1)}, bf16[1,32,512]{2,1,0:T(8,128)(2,1)}, u32[]{:S(2)}) copy-start(bf16[1,32,512]{2,1,0:T(8,128)(2,1)} %get-tuple-element.19) | copy-start | bytes 98308

commit v3 on v2

--- a/solution.py
+++ b/solution.py
@@ -61,19 +61,19 @@
 
 
 class Gather:
-    def __init__(self, place, parts, send, recv, direct, far):
+    def __init__(self, place, parts, send, recv, direct, far, over):
         self.place, self.parts, self.send, self.recv = place, parts, send, recv
-        self.direct, self.far = direct, far
+        self.direct, self.far, self.over = direct, far, over
         self.peer = {
             (axis, step): place.at(axis, step) for axis in ("x", "y", "z") for step in (1, -1, 2)
         }
 
-    def piece(self, k, dz, du=0, dv=0, many=None):
-        ref, first, columns, u, v = self.parts[k]
-        spot = {u: self.place.on(u, du), v: self.place.on(v, dv)}
+    def piece(self, k, da, du=0, dv=0, many=None):
+        ref, first, columns, a, u, v = self.parts[k]
+        spot = {a: self.place.on(a, da), u: self.place.on(u, du), v: self.place.on(v, dv)}
         if many is not None:
             spot[u] = many
-        return ref.at[self.place.on("z", dz), spot["y"], spot["x"], :, pl.ds(first, columns)]
+        return ref.at[spot["z"], spot["y"], spot["x"], :, pl.ds(first, columns)]
 
     def copy(self, k, piece, axis, step, slot):
         stage = 0 if slot < 3 else 1 if slot < 15 else 2
@@ -86,28 +86,30 @@
             device_id_type=MESH,
         )
 
-    def along_z(self, k, start):
+    def along_a(self, k, start):
+        a = self.parts[k][3]
         for step in (1, -1):
-            copy = self.copy(k, self.piece(k, 0 if start else -step), "z", step, (1 - step) // 2)
+            copy = self.copy(k, self.piece(k, 0 if start else -step), a, step, (1 - step) // 2)
             copy.start() if start else copy.wait_recv()
 
-    def past_z(self, k, start):
+    def past_a(self, k, start):
+        a = self.parts[k][3]
         step = 1 if k % 2 else -1
         source = -step
         if self.far:
             step, source = 2, 0
-        copy = self.copy(k, self.piece(k, source if start else 2), "z", step, 2)
+        copy = self.copy(k, self.piece(k, source if start else 2), a, step, 2)
         copy.start() if start else copy.wait_recv()
 
     def along_u(self, k, dz, start):
-        u = self.parts[k][3]
+        u = self.parts[k][4]
         for step in (1, -1):
             piece = self.piece(k, dz, 0 if start else -step)
             copy = self.copy(k, piece, u, step, 3 + 3 * (dz % RING) + (1 - step) // 2)
             copy.start() if start else copy.wait_recv()
 
     def past_u(self, k, dz, start):
-        u = self.parts[k][3]
+        u = self.parts[k][4]
         step = 1 if dz % 2 else -1
         source = -step
         if dz % RING in self.direct:
@@ -117,14 +119,19 @@
         copy.start() if start else copy.wait_recv()
 
     def along_v(self, k, dz, start):
-        v = self.parts[k][4]
+        v = self.parts[k][5]
         for step in (1, -1):
             piece = self.piece(k, dz, 0, 0 if start else -step, slice(0, RING))
             copy = self.copy(k, piece, v, step, 15 + 4 * (dz % RING) + (1 - step) // 2)
             copy.start() if start else copy.wait_recv()
 
     def past_v(self, k, dz, start):
-        v = self.parts[k][4]
+        v = self.parts[k][5]
+        if dz % RING in self.over:
+            piece = self.piece(k, dz, 0, 0 if start else 2, slice(0, RING))
+            copy = self.copy(k, piece, v, 2, 17 + 4 * (dz % RING))
+            copy.start() if start else copy.wait_recv()
+            return
         for step in (1, -1):
             half = slice(0, 2) if step == 1 else slice(2, RING)
             piece = self.piece(k, dz, 0, -step if start else 2, half)
@@ -144,19 +151,22 @@
     def send_v(self, k, dz):
         self.past_u(k, dz, False)
         self.along_v(k, dz, True)
+        if dz % RING in self.over:
+            self.past_v(k, dz, True)
 
     def take_v(self, k, dz):
         self.along_v(k, dz, False)
-        self.past_v(k, dz, True)
+        if dz % RING not in self.over:
+            self.past_v(k, dz, True)
 
     def begin(self, parts):
         for k in parts:
-            self.along_z(k, True)
+            self.along_a(k, True)
         for k in parts:
             self.send_u(k, 0)
         for k in parts:
             if self.far:
-                self.past_z(k, True)
+                self.past_a(k, True)
 
     def finish(self, parts):
         def each(step, *planes):
@@ -167,14 +177,14 @@
         each(self.take_u, 0)
         each(self.send_v, 0)
         for k in parts:
-            self.along_z(k, False)
+            self.along_a(k, False)
             if not self.far:
-                self.past_z(k, True)
+                self.past_a(k, True)
         each(self.send_u, -1, 1)
         each(self.take_u, -1, 1)
         each(self.take_v, 0)
         for k in parts:
-            self.past_z(k, False)
+            self.past_a(k, False)
         each(self.send_u, 2)
         each(self.send_v, -1, 1)
         each(self.take_u, 2)
@@ -377,7 +387,7 @@
         tag = jnp.broadcast_to(tags[:1, :], (TOKENS, TOKENS))
         row = lax.broadcasted_iota(jnp.int32, (TOKENS, TOKENS), 0)
         col = lax.broadcasted_iota(jnp.int32, (TOKENS, TOKENS), 1)
-        return (tag == tag.T) & (row // 32 == col // 32) & (row >= col)
+        return (tag == tag.T) & (row // 32 == col // 32) & (row <= col)
 
     def project():
         @pl.when(section == 0)
@@ -416,20 +426,19 @@
         q[...] = (wide[:, :QW] * r).astype(BF)
         kv[...] = (wide[:, QW : QW + KVW] * r).astype(BF)
 
-        mask = allowed()
+        mask = jnp.concatenate([allowed()] * 4, axis=1)
         for group in range(4):
             start = (group // 2) * 128
             keys = both_halves(kv[:, start : start + 128], group % 2)
             values = both_halves(kv[:, 256 + start : 256 + start + 128], group % 2)
-            score = mm(head_rows(q, group), keys, NT).reshape(4, TOKENS, TOKENS)
-            weight = jnp.where(mask[None], jnp.exp(score * (HEAD**-0.5)), 0.0)
-            prob = weight / jnp.sum(weight, axis=-1, keepdims=True)
-            prob = prob.reshape(4 * TOKENS, TOKENS)
+            score = mm(keys, head_rows(q, group), NT)
+            weight = jnp.where(mask, jnp.exp(score * (HEAD**-0.5)), 0.0)
+            prob = weight / jnp.sum(weight, axis=0, keepdims=True)
             probs[group] = prob
 
             @pl.when(section < last)
             def _():
-                put_heads(mixed, group, mm(prob.astype(BF), values))
+                put_heads(mixed, group, mm(prob.astype(BF), values, TN))
 
     def prepare():
         def turn(i, carry):
@@ -481,23 +490,26 @@
     weights = Gather(
         place,
         [
-            (wq, 0, QW // 2, "x", "y"),
-            (wq, QW // 2, QW // 2, "y", "x"),
-            (wo, 0, WIDTH // 2, "x", "y"),
-            (wo, WIDTH // 2, WIDTH // 2, "y", "x"),
+            (wq, 0, 384, "z", "x", "y"),
+            (wq, 384, 384, "z", "y", "x"),
+            (wq, 768, 256, "x", "y", "z"),
+            (wo, 0, 896, "z", "x", "y"),
+            (wo, 896, 896, "z", "y", "x"),
+            (wo, 1792, 256, "y", "x", "z"),
         ],
         w_send,
         w_recv,
+        (0,),
+        False,
         (),
-        False,
     )
     wq[place.z, place.y, place.x] = wq_share[0]
     wo[place.z, place.y, place.x] = wo_share[0]
 
-    weights.begin((0, 1, 2, 3))
+    weights.begin(range(6))
     for i in range(RING):
         tags[:1, i * 32 : (i + 1) * 32] = docs[0, pl.ds(plan[0, i], 1), :].astype(F32)
-    weights.finish((0, 1, 2, 3))
+    weights.finish(range(6))
 
     load_wait()
 
@@ -529,12 +541,12 @@
         heads = head_rows(q, group)
         heads_grad = head_rows(mixed_grad, group)
         prob = probs[group]
-        prob_grad = mm(heads_grad, values, NT)
-        inner = jnp.sum(prob_grad * prob, axis=-1, keepdims=True)
+        prob_grad = mm(values, heads_grad, NT)
+        inner = jnp.sum(prob_grad * prob, axis=0, keepdims=True)
         score_grad = (prob * (prob_grad - inner) * (HEAD**-0.5)).astype(BF)
-        put_heads(dq, group, mm(score_grad, keys))
-        dk = mm(score_grad, heads, TN)
-        dv = mm(prob.astype(BF), heads_grad, TN)
+        put_heads(dq, group, mm(score_grad, keys, TN))
+        dk = mm(score_grad, heads)
+        dv = mm(prob.astype(BF), heads_grad)
         folded.append((dk + pltpu.roll(dk, HEAD, 1), dv + pltpu.roll(dv, HEAD, 1)))
         if group % 2 == 1:
             for part in range(2):
@@ -608,7 +620,18 @@
         grads = grads + z_all[src].astype(F32)
     grads = grads * (1.0 / REPLICAS)
     outputs = Gather(
-        place, [(stash_out, 0, KVW, "x", "y"), (next_out, 0, KVW, "y", "x")], o_send, o_recv, (0, 1, 2, 3), True
+        place,
+        [
+            (stash_out, 0, 384, "z", "x", "y"),
+            (next_out, 0, 384, "z", "y", "x"),
+            (stash_out, 384, 128, "x", "y", "z"),
+            (next_out, 384, 128, "y", "x", "z"),
+        ],
+        o_send,
+        o_recv,
+        (0, 1, 2, 3),
+        True,
+        (2,),
     )
     own = pl.ds(pl.multiple_of(place.me * 32, 32), 32)
     rows = kv_now[0, own, :]
@@ -620,14 +643,32 @@
         moved = rows.astype(F32) - learn_rate * first_new / (jnp.sqrt(second_new) + adam_eps)
         rows, first, second = moved.astype(BF), first_new.astype(BF), second_new.astype(BF)
         target[place.z, place.y, place.x] = rows
-        outputs.begin((step,))
+        outputs.begin((step, step + 2))
     m_out[0] = first
     v_out[0] = second
-    outputs.finish((0, 1))
+    outputs.finish(range(4))
 
     weights.drain()
     outputs.drain()
     drain_hops()
+
+
+def place_results(*refs):
+    sem = refs[12]
+    loads, stores = [], []
+    for i in range(4):
+        for part in range(RING if i < 2 else 1):
+            slot = len(loads)
+            src, dst, held = (refs[j + i].at[part] for j in (0, 4, 8))
+            loads.append(pltpu.make_async_copy(src, held, sem.at[0, slot]))
+            stores.append(pltpu.make_async_copy(held, dst, sem.at[1, slot]))
+    for load in loads:
+        load.start()
+    for load, store in zip(loads, stores):
+        load.wait()
+        store.start()
+    for store in stores:
+        store.wait()
 
 
 def body(
@@ -639,7 +680,7 @@
     dma = pltpu.SemaphoreType.DMA
     version = jax.ShapeDtypeStruct((RING, RING, RING, 32, KVW), BF)
     moment = jax.ShapeDtypeStruct((1, 32, KVW), BF)
-    stash, current, first, second = pl.pallas_call(
+    results = pl.pallas_call(
         kernel,
         out_shape=(version, version, moment, moment),
         in_specs=[hbm, hbm, smem, vmem, vmem, vmem, vmem, hbm, hbm, vmem, vmem],
@@ -664,7 +705,7 @@
             pltpu.VMEM((TOKENS, 128), F32),
             pltpu.VMEM((TOKENS, QW), BF),
             pltpu.VMEM((TOKENS, KVW), BF),
-            pltpu.VMEM((4, 4 * TOKENS, TOKENS), F32),
+            pltpu.VMEM((4, TOKENS, 4 * TOKENS), F32),
             pltpu.VMEM((TOKENS, QW), BF),
             pltpu.VMEM((TOKENS, QW), BF),
             pltpu.VMEM((TOKENS, QW), BF),
@@ -680,10 +721,10 @@
             pltpu.VMEM((RING, 2, 32, 2 * KVW), BF),
             pltpu.VMEM((RING, 32, 2 * KVW), BF),
             pltpu.VMEM((RING, 32, 2 * KVW), BF),
+            dma((6, 3)),
+            dma((6, 31)),
             dma((4, 3)),
             dma((4, 31)),
-            dma((2, 3)),
-            dma((2, 31)),
             dma((2, CHUNKS)),
             dma((2, CHUNKS)),
             dma((7, RING - 1)),
@@ -694,6 +735,15 @@
             collective_id=0, has_side_effects=True, vmem_limit_bytes=56 * 1024 * 1024
         ),
     )(embeddings, cotangent, plan, doc_ids, norm_gain, w_query, w_out, kv_stash, kv_now, adam_m, adam_v)
+    pieces = 2 * RING + 2
+    stash, current, first, second = pl.pallas_call(
+        place_results,
+        out_shape=[jax.ShapeDtypeStruct(r.shape, BF) for r in results],
+        in_specs=[hbm] * 4,
+        out_specs=[hbm] * 4,
+        scratch_shapes=[pltpu.VMEM(r.shape, BF) for r in results] + [dma((2, pieces))],
+        compiler_params=pltpu.CompilerParams(vmem_limit_bytes=60 * 1024 * 1024),
+    )(*results)
     shape = (1, WIDTH, KVW)
     return stash.reshape(shape), current.reshape(shape), first, second
 

time: 165 us -> 157 us (0.952)
  local copies, waits for them, and re-layouts: 5.75 us -> 0 us
  Pallas kernels: 158 us -> 156 us
    unnamed x10 -> x0, local copies, waits for them, and re-layouts: 5.75 us -> none
    pallas_call x1, Pallas kernels: 158 us -> 153 us  [body(): pl.pallas_call(kernel, out_shape=(version, version, moment, moment), in_s...]
    pallas_call x0 -> x1, Pallas kernels: none -> 3.62 us  [body(): pl.pallas_call(place_results, out_shape=[jax.ShapeDtypeStruct(r.shape, BF...]
where the time goes in v3:
time: 157 us
  Pallas kernels  156 us (99%)
    pallas_call x1, Pallas kernels, body(): pl.pallas_call(kernel, out_shape=(version, version, moment, moment), in_s...  153 us
    pallas_call x1, Pallas kernels, body(): pl.pallas_call(place_results, out_shape=[jax.ShapeDtypeStruct(r.shape, BF...  3.62 us

profile of v3, /device:TPU:2, one launch (start us, length us, event | category | flops | bytes accessed | tf_op | source)
XLA Modules:
  0.0 157.2 jit_solution(10465427302138453416)
XLA Ops:
  0.6 152.8 %shard_map.138 = (bf16[4,4,4,32,512]{4,3,2,1,0:T(8,128)(2,1)}, bf16[4,4,4,32,512]{4,3,2,1,0:T(8,128)(2,1)}, bf16[1,32,512]{2,1,0:T(8,128)(2,1)}, bf16[1,32,512]{2,1,0:T(8,128)(2,1)}) custom-call(bf16[1,4,32,2048]{3,2,1,0:T(8,128)(2,1)} %emb_in.1, bf16[1,4,32,2048]{3,2,1,0:T(8,128)(2,1)} %cot_in.1, s32[1,4]{1,0:T(1,128)} %plan.1, s32[1,4,32]{2,1,0:T(4,128)} %docs.1, ...), custom_call_target="tpu_custom_call" | custom-call | tf_op jit(solution)/shard_map/pallas_call | solution.py:683
  153.5 3.6 %shard_map.139 = (bf16[4,4,4,32,512]{4,3,2,1,0:T(8,128)(2,1)}, bf16[4,4,4,32,512]{4,3,2,1,0:T(8,128)(2,1)}, bf16[1,32,512]{2,1,0:T(8,128)(2,1)}, bf16[1,32,512]{2,1,0:T(8,128)(2,1)}) custom-call(bf16[4,4,4,32,512]{4,3,2,1,0:T(8,128)(2,1)} %get-tuple-element.12.refs_0_, bf16[4,4,4,32,512]{4,3,2,1,0:T(8,128)(2,1)} %get-tuple-element.13.refs_1_, ...), custom_call_target="tpu_custom_call" | custom-call | tf_op jit(solution)/shard_map/pallas_call | solution.py:739

commit v4 on v3

--- a/solution.py
+++ b/solution.py
@@ -181,14 +181,19 @@
             if not self.far:
                 self.past_a(k, True)
         each(self.send_u, -1, 1)
-        each(self.take_u, -1, 1)
-        each(self.take_v, 0)
+        if not self.far:
+            each(self.take_u, -1, 1)
+            each(self.take_v, 0)
         for k in parts:
             self.past_a(k, False)
         each(self.send_u, 2)
+        if self.far:
+            each(self.take_u, -1, 1)
         each(self.send_v, -1, 1)
         each(self.take_u, 2)
         each(self.send_v, 2)
+        if self.far:
+            each(self.take_v, 0)
         each(self.take_v, -1, 1, 2)
         each(lambda k, dz: self.past_v(k, dz, False), 0, -1, 1, 2)
 
@@ -311,6 +316,7 @@
     n_x,
     k_y,
     k_x,
+    lefts,
     x_buf,
     x_all,
     y_buf,
@@ -583,17 +589,22 @@
     def _():
         share_normed()
 
-    for one in n_trades + k_trades:
-        one.wait()
     token = lax.broadcasted_iota(jnp.int32, (256, RING * TOKENS), 1)
     early = lax.rem(token, TOKENS) < HALF
-    for n_all, k_all, buf in ((n_y, k_y, x_buf), (n_x, k_x, y_buf)):
+    for one in n_trades:
+        one.wait()
+    for half, n_all in enumerate((n_y, n_x)):
         left = jnp.concatenate([n_all[src].reshape(256, TOKENS) for src in range(RING)], axis=1)
+        zero = jnp.zeros_like(left)
+        lefts[half, 0] = jnp.where(early, left, zero)
+        lefts[half, 1] = jnp.where(early, zero, left)
+    weights.drain()
+    for one in k_trades:
+        one.wait()
+    for half, k_all, buf in ((0, k_y, x_buf), (1, k_x, y_buf)):
         right = k_all[...].reshape(RING * TOKENS, KVW)
-        zero = jnp.zeros_like(left)
         for step in range(2):
-            own = jnp.where(early, left, zero) if step == 0 else jnp.where(early, zero, left)
-            part = mm(own, right).astype(BF).reshape(2, RING, 32, KVW)
+            part = mm(lefts[half, step], right).astype(BF).reshape(2, RING, 32, KVW)
             for there in range(RING):
                 buf[there, :, :, step * KVW : (step + 1) * KVW] = part[:, there]
         one = (
@@ -648,7 +659,6 @@
     v_out[0] = second
     outputs.finish(range(4))
 
-    weights.drain()
     outputs.drain()
     drain_hops()
 
@@ -715,6 +725,7 @@
             pltpu.VMEM((RING, 2, RING, 32, TOKENS), BF),
             pltpu.VMEM((RING, TOKENS, KVW), BF),
             pltpu.VMEM((RING, TOKENS, KVW), BF),
+            pltpu.VMEM((2, 2, 256, RING * TOKENS), BF),
             pltpu.VMEM((RING, 2, 32, 2 * KVW), BF),
             pltpu.VMEM((RING, 2, 32, 2 * KVW), BF),
             pltpu.VMEM((RING, 2, 32, 2 * KVW), BF),

time: 157 us -> 158 us (level); the launches traced: 157 us -> 156 us
  no operation moved by 1% of the time
where the time goes in v4:
time: 158 us; the launch traced here: 156 us
  Pallas kernels  155 us (98%)
    pallas_call x1, Pallas kernels, body(): pl.pallas_call(kernel, out_shape=(version, version, moment, moment), in_s...  151 us
    pallas_call x1, Pallas kernels, body(): pl.pallas_call(place_results, out_shape=[jax.ShapeDtypeStruct(r.shape, BF...  3.62 us

profile of v4, /device:TPU:2, one launch (start us, length us, event | category | flops | bytes accessed | tf_op | source)
XLA Modules:
  0.0 155.7 jit_solution(5808689627371411207)
XLA Ops:
  0.6 151.2 %shard_map.138 = (bf16[4,4,4,32,512]{4,3,2,1,0:T(8,128)(2,1)}, bf16[4,4,4,32,512]{4,3,2,1,0:T(8,128)(2,1)}, bf16[1,32,512]{2,1,0:T(8,128)(2,1)}, bf16[1,32,512]{2,1,0:T(8,128)(2,1)}) custom-call(bf16[1,4,32,2048]{3,2,1,0:T(8,128)(2,1)} %emb_in.1, bf16[1,4,32,2048]{3,2,1,0:T(8,128)(2,1)} %cot_in.1, s32[1,4]{1,0:T(1,128)} %plan.1, s32[1,4,32]{2,1,0:T(4,128)} %docs.1, ...), custom_call_target="tpu_custom_call" | custom-call | tf_op jit(solution)/shard_map/pallas_call | solution.py:693
  151.9 3.6 %shard_map.139 = (bf16[4,4,4,32,512]{4,3,2,1,0:T(8,128)(2,1)}, bf16[4,4,4,32,512]{4,3,2,1,0:T(8,128)(2,1)}, bf16[1,32,512]{2,1,0:T(8,128)(2,1)}, bf16[1,32,512]{2,1,0:T(8,128)(2,1)}) custom-call(bf16[4,4,4,32,512]{4,3,2,1,0:T(8,128)(2,1)} %get-tuple-element.12.refs_0_, bf16[4,4,4,32,512]{4,3,2,1,0:T(8,128)(2,1)} %get-tuple-element.13.refs_1_, ...), custom_call_target="tpu_custom_call" | custom-call | tf_op jit(solution)/shard_map/pallas_call | solution.py:750

commit v5 on v4

--- a/solution.py
+++ b/solution.py
@@ -168,7 +168,7 @@
             if self.far:
                 self.past_a(k, True)
 
-    def finish(self, parts):
+    def finish(self, parts, settle=None):
         def each(step, *planes):
             for dz in planes:
                 for k in parts:
@@ -195,7 +195,16 @@
         if self.far:
             each(self.take_v, 0)
         each(self.take_v, -1, 1, 2)
-        each(lambda k, dz: self.past_v(k, dz, False), 0, -1, 1, 2)
+        for dz in (0, -1, 1, 2):
+            for k in parts:
+                self.past_v(k, dz, False)
+                if settle is not None:
+                    settle(k, dz).start()
+
+    def plane(self, k, dz, ref):
+        first, columns, a = self.parts[k][1:4]
+        spot = [self.place.on(a, dz) if axis == a else slice(0, RING) for axis in "zyx"]
+        return ref.at[spot[0], spot[1], spot[2], :, pl.ds(first, columns)]
 
     def drain(self):
         for k in range(len(self.parts)):
@@ -287,6 +296,8 @@
     next_out,
     m_out,
     v_out,
+    stash_all,
+    next_all,
     emb,
     cot,
     kv_stash,
@@ -332,6 +343,7 @@
     trade_send,
     trade_recv,
     load_sem,
+    settle_sem,
 ):
     place = Place()
     section = lax.axis_index("section")
@@ -633,10 +645,10 @@
     outputs = Gather(
         place,
         [
-            (stash_out, 0, 384, "z", "x", "y"),
-            (next_out, 0, 384, "z", "y", "x"),
-            (stash_out, 384, 128, "x", "y", "z"),
-            (next_out, 384, 128, "y", "x", "z"),
+            (stash_all, 0, 384, "z", "x", "y"),
+            (next_all, 0, 384, "z", "y", "x"),
+            (stash_all, 384, 128, "x", "y", "z"),
+            (next_all, 384, 128, "y", "x", "z"),
         ],
         o_send,
         o_recv,
@@ -647,7 +659,7 @@
     own = pl.ds(pl.multiple_of(place.me * 32, 32), 32)
     rows = kv_now[0, own, :]
     first, second = adam_m[0], adam_v[0]
-    for step, target in ((0, stash_out), (1, next_out)):
+    for step, target in ((0, stash_all), (1, next_all)):
         grad = grads[:, step * KVW : (step + 1) * KVW]
         first_new = beta_first * first.astype(F32) + (1.0 - beta_first) * grad
         second_new = beta_second * second.astype(F32) + (1.0 - beta_second) * grad * grad
@@ -657,7 +669,16 @@
         outputs.begin((step, step + 2))
     m_out[0] = first
     v_out[0] = second
-    outputs.finish(range(4))
+    def settle(k, dz):
+        full, out = ((stash_all, stash_out), (next_all, next_out))[k % 2]
+        return pltpu.make_async_copy(
+            outputs.plane(k, dz, full), outputs.plane(k, dz, out), settle_sem.at[k, dz % RING]
+        )
+
+    outputs.finish(range(4), settle)
+    for dz in (0, -1, 1, 2):
+        for k in range(4):
+            settle(k, dz).wait()
 
     outputs.drain()
     drain_hops()
@@ -694,8 +715,10 @@
         kernel,
         out_shape=(version, version, moment, moment),
         in_specs=[hbm, hbm, smem, vmem, vmem, vmem, vmem, hbm, hbm, vmem, vmem],
-        out_specs=(vmem,) * 4,
+        out_specs=(hbm, hbm, vmem, vmem),
         scratch_shapes=[
+            pltpu.VMEM((RING, RING, RING, 32, KVW), BF),
+            pltpu.VMEM((RING, RING, RING, 32, KVW), BF),
             pltpu.VMEM((1, 4, 32, WIDTH), BF),
             pltpu.VMEM((1, 4, 32, WIDTH), BF),
             pltpu.VMEM((1, WIDTH, KVW), BF),
@@ -741,6 +764,7 @@
             dma((7, RING - 1)),
             dma((7, RING - 1)),
             dma((4,)),
+            dma((4, RING)),
         ],
         compiler_params=pltpu.CompilerParams(
             collective_id=0, has_side_effects=True, vmem_limit_bytes=56 * 1024 * 1024

time: 158 us -> 157 us (level)
  no operation moved by 1% of the time
where the time goes in v5:
time: 157 us; the launch traced here: 155 us
  Pallas kernels  155 us (99%)
    pallas_call x1, Pallas kernels, body(): pl.pallas_call(kernel, out_shape=(version, version, moment, moment), in_s...  151 us
    pallas_call x1, Pallas kernels, body(): pl.pallas_call(place_results, out_shape=[jax.ShapeDtypeStruct(r.shape, BF...  3.62 us

profile of v5, /device:TPU:2, one launch (start us, length us, event | category | flops | bytes accessed | tf_op | source)
XLA Modules:
  0.0 155.4 jit_solution(16413176014954951186)
XLA Ops:
  0.6 151.0 %shard_map.138 = (bf16[4,4,4,32,512]{4,3,2,1,0:T(8,128)(2,1)}, bf16[4,4,4,32,512]{4,3,2,1,0:T(8,128)(2,1)}, bf16[1,32,512]{2,1,0:T(8,128)(2,1)}, bf16[1,32,512]{2,1,0:T(8,128)(2,1)}) custom-call(bf16[1,4,32,2048]{3,2,1,0:T(8,128)(2,1)} %emb_in.1, bf16[1,4,32,2048]{3,2,1,0:T(8,128)(2,1)} %cot_in.1, s32[1,4]{1,0:T(1,128)} %plan.1, s32[1,4,32]{2,1,0:T(4,128)} %docs.1, ...), custom_call_target="tpu_custom_call" | custom-call | tf_op jit(solution)/shard_map/pallas_call | solution.py:714
  151.6 3.6 %shard_map.139 = (bf16[4,4,4,32,512]{4,3,2,1,0:T(8,128)(2,1)}, bf16[4,4,4,32,512]{4,3,2,1,0:T(8,128)(2,1)}, bf16[1,32,512]{2,1,0:T(8,128)(2,1)}, bf16[1,32,512]{2,1,0:T(8,128)(2,1)}) custom-call(bf16[4,4,4,32,512]{4,3,2,1,0:T(8,128)(2,1)} %get-tuple-element.12.refs_0_, bf16[4,4,4,32,512]{4,3,2,1,0:T(8,128)(2,1)} %get-tuple-element.13.refs_1_, ...), custom_call_target="tpu_custom_call" | custom-call | tf_op jit(solution)/shard_map/pallas_call | solution.py:774
